TPU v7x, 32 devices: a whole 2x2x4 slice. The times are simulated.
32 devices in a mesh: gx: 8 (over z, core), gy: 4 (over y, x).
Axes of the slice: x: 2, y: 2, z: 4, core: 2. Of those that a mesh axis runs over, the one named last changes fastest.
Arguments:
- fields: float32 [2, 512, 1024], P(None, 'gy', 'gx'), may hold values from -8 to 8
- material: int32 [512, 1024], P('gy', 'gx'), may hold values from 0 to 7
- conduct: float32 [2, 8], replicated, may hold values from 0.25 to 4
- joints_x: int32 [512, 8], P('gy'), may hold values from 1 to 1023
- joints_y: int32 [1024, 8], P('gx'), may hold values from 1 to 511
Outputs:
- half_step: float32 [2, 512, 1024], P(None, 'gy', 'gx')
- advanced: float32 [2, 512, 1024], P(None, 'gy', 'gx')
Inputs may be any that keep to these rules, and one draw needn't show every extreme that they name: `joints_x`: entries of one row may repeat. `joints_y`: entries of one column may repeat.
All inputs are finite; a program needn't handle non-finite values.
Results may differ from a plain program's by a relative error of at most 0.0015.
Values sent between devices are 32-bit elements; how exact they have to be, the bound alone decides.
A program may use at most 64 MiB of HBM per device.

v0:
```python
import jax
import jax.numpy as jnp
from jax import lax
from jax.sharding import PartitionSpec as P

MATERIALS = 8
FOURIER = 8192
DRYING = 4096


def with_halo(block, sides, width):
    for axis, dim in sides:
        count = lax.axis_size(axis)
        forward = [(i, i + 1) for i in range(count - 1)]
        backward = [(target, source) for source, target in forward]
        low = lax.ppermute(
            lax.slice_in_dim(block, block.shape[dim] - width, None, axis=dim), axis, forward
        )
        high = lax.ppermute(lax.slice_in_dim(block, 0, width, axis=dim), axis, backward)
        block = jnp.concatenate([low, block, high], axis=dim)
    return block


def shifted(array_in, stride, line_axis, fill_value, earlier):
    length = array_in.shape[line_axis]
    filler = jnp.full(
        array_in.shape[:line_axis] + (stride,) + array_in.shape[line_axis + 1 :],
        fill_value,
        array_in.dtype,
    )
    if earlier:
        return jnp.concatenate(
            [filler, lax.slice_in_dim(array_in, 0, length - stride, axis=line_axis)], line_axis
        )
    return jnp.concatenate(
        [lax.slice_in_dim(array_in, stride, length, axis=line_axis), filler], line_axis
    )


def cyclic(lower, diagonal, upper, sides, line_axis):
    length = diagonal.shape[line_axis]
    for rounds in range((length - 1).bit_length()):
        stride = 1 << rounds
        before_gain = -lower / shifted(diagonal, stride, line_axis, 1.0, True)
        after_gain = -upper / shifted(diagonal, stride, line_axis, 1.0, False)
        new_diagonal = (
            diagonal
            + before_gain * shifted(upper, stride, line_axis, 0.0, True)
            + after_gain * shifted(lower, stride, line_axis, 0.0, False)
        )
        sides = tuple(
            (
                entry
                + before_gain * shifted(entry, stride, line_axis, 0.0, True)
                + after_gain * shifted(entry, stride, line_axis, 0.0, False)
                for entry in sides
            )
        )
        lower = before_gain * shifted(lower, stride, line_axis, 0.0, True)
        upper = after_gain * shifted(upper, stride, line_axis, 0.0, False)
        diagonal = new_diagonal
    return tuple((entry / diagonal for entry in sides))


def per_device(fields, material, conduct, joints_x, joints_y):
    row_count, col_count = material.shape
    conduction = jnp.zeros((2, row_count, col_count), jnp.float32)
    for klass in range(MATERIALS):
        conduction = jnp.where(
            material[None] == klass, conduct[:, klass][:, None, None], conduction
        )
    padded = with_halo(conduction, (("gx", 2), ("gy", 1)), 1)
    center = padded[:, 1:-1, 1:-1]
    col_pos = lax.axis_index("gx") * col_count + jnp.arange(col_count, dtype=jnp.int32)
    row_pos = lax.axis_index("gy") * row_count + jnp.arange(row_count, dtype=jnp.int32)
    width_total = col_count * lax.axis_size("gx")
    height_total = row_count * lax.axis_size("gy")
    face_scale = jnp.array([FOURIER, DRYING], jnp.float32)[:, None, None]
    cut_west = jnp.any(joints_x[:, None, :] == col_pos[None, :, None], axis=2).astype(jnp.float32)
    cut_east = jnp.any(joints_x[:, None, :] == col_pos[None, :, None] + 1, axis=2).astype(
        jnp.float32
    )
    cut_north = jnp.any(joints_y[None, :, :] == row_pos[:, None, None], axis=2).astype(jnp.float32)
    cut_south = jnp.any(joints_y[None, :, :] == row_pos[:, None, None] + 1, axis=2).astype(
        jnp.float32
    )
    west_face = jnp.where(
        col_pos > 0, face_scale * 0.5 * (padded[:, 1:-1, :-2] + center) * (1.0 - cut_west), 0.0
    )
    east_face = jnp.where(
        col_pos < width_total - 1,
        face_scale * 0.5 * (center + padded[:, 1:-1, 2:]) * (1.0 - cut_east),
        0.0,
    )
    north_face = jnp.where(
        row_pos[:, None] > 0,
        face_scale * 0.5 * (padded[:, :-2, 1:-1] + center) * (1.0 - cut_north),
        0.0,
    )
    south_face = jnp.where(
        row_pos[:, None] < height_total - 1,
        face_scale * 0.5 * (center + padded[:, 2:, 1:-1]) * (1.0 - cut_south),
        0.0,
    )
    values = lax.all_to_all(fields, "gx", split_axis=1, concat_axis=2, tiled=True)
    low_face = lax.all_to_all(west_face, "gx", split_axis=1, concat_axis=2, tiled=True)
    high_face = lax.all_to_all(east_face, "gx", split_axis=1, concat_axis=2, tiled=True)
    solved = cyclic(-low_face, 1.0 + low_face + high_face, -high_face, (values,), 2)[0]
    half_step = lax.all_to_all(solved, "gx", split_axis=2, concat_axis=1, tiled=True)
    values = lax.all_to_all(half_step, "gy", split_axis=2, concat_axis=1, tiled=True)
    low_face = lax.all_to_all(north_face, "gy", split_axis=2, concat_axis=1, tiled=True)
    high_face = lax.all_to_all(south_face, "gy", split_axis=2, concat_axis=1, tiled=True)
    solved = cyclic(-low_face, 1.0 + low_face + high_face, -high_face, (values,), 1)[0]
    advanced = lax.all_to_all(solved, "gy", split_axis=1, concat_axis=2, tiled=True)
    return (half_step, advanced)


def solution(mesh):
    return jax.shard_map(
        per_device,
        mesh=mesh,
        in_specs=(P(None, "gy", "gx"), P("gy", "gx"), P(), P("gy", None), P("gx", None)),
        out_specs=(P(None, "gy", "gx"), P(None, "gy", "gx")),
        check_vma=False,
    )
```

profile of v0, /device:TPU:0, one launch (start us, length us, event | category | flops | bytes accessed | tf_op | source)
XLA Modules:
  0.0 120.0 jit_solution(5625619011226960867)
XLA Ops:
  2.6 2.4 %collective-permute-start = (f32[2,128,1]{2,0,1:T(2,128)S(1)}, f32[2,128,1]{2,0,1:T(2,128)S(1)}, u32[]{:S(2)}, u32[]{:S(2)}) collective-permute-start(f32[2,128,1]{2,0,1:T(2,128)S(1)} %get-tuple-element.230), channel_id=1, source_target_pairs={{0,4},{4,8},{8,12},{12,16},{16,20},{20,24},{24,28},{1,5},{5,9},{9,... | collective-permute-start | bytes 3080 | tf_op jit(solution)/shard_map/ppermute | solution.py:16
  5.0 1.3 %collective-permute-start.1 = (f32[2,128,1]{2,0,1:T(2,128)S(1)}, f32[2,128,1]{2,0,1:T(2,128)S(1)}, u32[]{:S(2)}, u32[]{:S(2)}) collective-permute-start(f32[2,128,1]{2,0,1:T(2,128)S(1)} %get-tuple-element.231), channel_id=1, source_target_pairs={{4,0},{8,4},{12,8},{16,12},{20,16},{24,20},{28,24},{5,1},{9,5},{13... | collective-permute-start | bytes 3080 | tf_op jit(solution)/shard_map/ppermute | solution.py:19
  8.7 1.7 %collective-permute-done.1 = f32[2,128,1]{2,0,1:T(2,128)S(1)} collective-permute-done((f32[2,128,1]{2,0,1:T(2,128)S(1)}, f32[2,128,1]{2,0,1:T(2,128)S(1)}, u32[]{:S(2)}, u32[]{:S(2)}) %collective-permute-start.1) | collective-permute-done | bytes 1056 | tf_op jit(solution)/shard_map/ppermute | solution.py:19
  10.5 3.4 %collective-permute-start.2 = (f32[2,1,130]{2,0,1:T(2,128)S(1)}, f32[2,1,130]{2,0,1:T(2,128)S(1)}, u32[]{:S(2)}, u32[]{:S(2)}) collective-permute-start(f32[2,1,130]{2,0,1:T(2,128)S(1)} %get-tuple-element.73), channel_id=1, source_target_pairs={{0,1},{1,2},{2,3},{4,5},{5,6},{6,7},{8,9},{9,10},{10,11},{12,13},{... | collective-permute-start | bytes 3128 | tf_op jit(solution)/shard_map/ppermute | solution.py:16
  13.9 1.3 %collective-permute-start.3 = (f32[2,1,130]{2,0,1:T(2,128)S(1)}, f32[2,1,130]{2,0,1:T(2,128)S(1)}, u32[]{:S(2)}, u32[]{:S(2)}) collective-permute-start(f32[2,1,130]{2,0,1:T(2,128)S(1)} %get-tuple-element.74), channel_id=1, source_target_pairs={{1,0},{2,1},{3,2},{5,4},{6,5},{7,6},{9,8},{10,9},{11,10},{13,12},{... | collective-permute-start | bytes 3128 | tf_op jit(solution)/shard_map/ppermute | solution.py:19
  16.0 3.4 %collective-permute-done.3 = f32[2,1,130]{2,0,1:T(2,128)S(1)} collective-permute-done((f32[2,1,130]{2,0,1:T(2,128)S(1)}, f32[2,1,130]{2,0,1:T(2,128)S(1)}, u32[]{:S(2)}, u32[]{:S(2)}) %collective-permute-start.3) | collective-permute-done | bytes 1072 | tf_op jit(solution)/shard_map/ppermute | solution.py:19
  20.0 1.8 %broadcast_select_fusion.1 = (f32[2,128,128]{2,0,1:T(2,128)S(1)}, f32[2,128,128]{2,0,1:T(2,128)S(1)}, f32[2,128,128]{2,0,1:T(2,128)}) fusion(pred[128]{0:T(512)(128)(4,1)S(1)} %get-tuple-element.245, f32[2,128,128]{2,0,1:T(2,128)S(1)} %select_select_fusion, f32[2,128,1]{2,0,1:T(2,128)S(1)} %collective-permute-done.1, ...), kind=kLoop, calls=%fused_computation.140 | loop fusion | flops 622592 | bytes 725416 | tf_op jit(solution)/shard_map/jit(_where)/select_n | solution.py:95
  22.5 3.7 %all-to-all-start.5 = ((f32[2,128,128]{1,0,2:T(2,128)}), f32[2,128,128]{1,0,2:T(2,128)S(1)}, u32[]{:S(2)}, u32[]{:S(2)}) async-start(f32[2,128,128]{1,0,2:T(2,128)} %copy.74), calls=%async_computation.5 | async-start | bytes 262144 | tf_op jit(solution)/shard_map/all_to_all | solution.py:111
  27.0 4.4 %all-to-all-done.5 = f32[2,128,128]{1,0,2:T(2,128)S(1)} async-done(((f32[2,128,128]{1,0,2:T(2,128)}), f32[2,128,128]{1,0,2:T(2,128)S(1)}, u32[]{:S(2)}, u32[]{:S(2)}) %all-to-all-start.5) | async-done | bytes 131104 | tf_op jit(solution)/shard_map/all_to_all | solution.py:111
  31.3 3.3 %all-to-all-start.6 = ((f32[2,128,128]{1,0,2:T(2,128)}), f32[2,128,128]{1,0,2:T(2,128)S(1)}, u32[]{:S(2)}, u32[]{:S(2)}) async-start(f32[2,128,128]{1,0,2:T(2,128)} %copy.77), calls=%async_computation.6 | async-start | bytes 262144 | tf_op jit(solution)/shard_map/all_to_all | solution.py:112
  35.6 4.4 %all-to-all-done.6 = f32[2,128,128]{1,0,2:T(2,128)S(1)} async-done(((f32[2,128,128]{1,0,2:T(2,128)}), f32[2,128,128]{1,0,2:T(2,128)S(1)}, u32[]{:S(2)}, u32[]{:S(2)}) %all-to-all-start.6) | async-done | bytes 131104 | tf_op jit(solution)/shard_map/all_to_all | solution.py:112
  39.9 6.2 %all-to-all-start = ((f32[2,128,128]{2,0,1:T(2,128)}), f32[2,128,128]{2,0,1:T(2,128)S(1)}, u32[]{:S(2)}, u32[]{:S(2)}) async-start(f32[2,128,128]{2,0,1:T(2,128)} %copy.61), calls=%async_computation | async-start | bytes 262144 | tf_op jit(solution)/shard_map/all_to_all | solution.py:105
  46.2 6.7 %all-to-all-done = f32[2,128,128]{2,0,1:T(2,128)S(1)} async-done(((f32[2,128,128]{2,0,1:T(2,128)}), f32[2,128,128]{2,0,1:T(2,128)S(1)}, u32[]{:S(2)}, u32[]{:S(2)}) %all-to-all-start) | async-done | bytes 131104 | tf_op jit(solution)/shard_map/all_to_all | solution.py:105
  52.9 3.4 %all-to-all-start.1 = ((f32[2,128,128]{2,0,1:T(2,128)}), f32[2,128,128]{2,0,1:T(2,128)S(1)}, u32[]{:S(2)}, u32[]{:S(2)}) async-start(f32[2,128,128]{2,0,1:T(2,128)} %fusion.12), calls=%async_computation.1 | async-start | bytes 262144 | tf_op jit(solution)/shard_map/all_to_all | solution.py:106
  56.5 6.5 %all-to-all-done.1 = f32[2,128,128]{2,0,1:T(2,128)S(1)} async-done(((f32[2,128,128]{2,0,1:T(2,128)}), f32[2,128,128]{2,0,1:T(2,128)S(1)}, u32[]{:S(2)}, u32[]{:S(2)}) %all-to-all-start.1) | async-done | bytes 131104 | tf_op jit(solution)/shard_map/all_to_all | solution.py:106
  63.0 3.4 %all-to-all-start.2 = ((f32[2,128,128]{2,0,1:T(2,128)}), f32[2,128,128]{2,0,1:T(2,128)S(1)}, u32[]{:S(2)}, u32[]{:S(2)}) async-start(f32[2,128,128]{2,0,1:T(2,128)} %get-tuple-element.75), calls=%async_computation.2 | async-start | bytes 262144 | tf_op jit(solution)/shard_map/all_to_all | solution.py:107
  66.5 6.6 %all-to-all-done.2 = f32[2,128,128]{2,0,1:T(2,128)S(1)} async-done(((f32[2,128,128]{2,0,1:T(2,128)}), f32[2,128,128]{2,0,1:T(2,128)S(1)}, u32[]{:S(2)}, u32[]{:S(2)}) %all-to-all-start.2) | async-done | bytes 131104 | tf_op jit(solution)/shard_map/all_to_all | solution.py:107
  79.6 2.1 %reshape.78 = f32[8,1,4096]{2,1,0:T(1,128)} reshape(f32[1024,2,16]{2,1,0:T(2,128)S(1)} %bitcast.91) | data formatting | bytes 262144
  81.7 3.4 %all-to-all-start.3 = ((f32[8,1,4096]{2,1,0:T(1,128)}), f32[8,1,4096]{2,1,0:T(1,128)S(1)}, u32[]{:S(2)}, u32[]{:S(2)}) async-start(f32[8,1,4096]{2,1,0:T(1,128)} %reshape.78), calls=%async_computation.3 | async-start | bytes 262144 | tf_op jit(solution)/shard_map/all_to_all | solution.py:109
  85.1 6.6 %all-to-all-done.3 = f32[8,1,4096]{2,1,0:T(1,128)S(1)} async-done(((f32[8,1,4096]{2,1,0:T(1,128)}), f32[8,1,4096]{2,1,0:T(1,128)S(1)}, u32[]{:S(2)}, u32[]{:S(2)}) %all-to-all-start.3) | async-done | bytes 131104 | tf_op jit(solution)/shard_map/all_to_all | solution.py:109
  93.1 1.4 %reshape.79 = f32[1024,2,16]{2,1,0:T(2,128)S(1)} reshape(f32[8,4096]{1,0:T(8,128)S(1)} %reduce.16) | data formatting | bytes 262144
  95.7 3.5 %all-to-all-start.4 = ((f32[2,128,128]{1,0,2:T(2,128)}), f32[2,128,128]{1,0,2:T(2,128)S(1)}, u32[]{:S(2)}, u32[]{:S(2)}) async-start(f32[2,128,128]{1,0,2:T(2,128)} %copy.71), calls=%async_computation.4 | async-start | bytes 262144 | tf_op jit(solution)/shard_map/all_to_all | solution.py:110
  99.3 4.7 %all-to-all-done.4 = f32[2,128,128]{1,0,2:T(2,128)S(1)} async-done(((f32[2,128,128]{1,0,2:T(2,128)}), f32[2,128,128]{1,0,2:T(2,128)S(1)}, u32[]{:S(2)}, u32[]{:S(2)}) %all-to-all-start.4) | async-done | bytes 131104 | tf_op jit(solution)/shard_map/all_to_all | solution.py:110
  110.2 7.4 %all_to_all.144 = f32[4,1,8192]{2,1,0:T(1,128)S(1)} all-to-all(f32[4,1,8192]{2,1,0:T(1,128)S(1)} %reshape.80), channel_id=1, replica_groups=mesh['gx'=8,'gy'=4] {'gy'}, dimensions={0} | all-to-all | bytes 262144 | tf_op jit(solution)/shard_map/all_to_all | solution.py:114
  (167 shorter events, 25.3 us)
Async XLA Ops:
  0.6 0.9 copy-start.2
  2.6 6.1 %collective-permute-start = (f32[2,128,1]{2,0,1:T(2,128)S(1)}, f32[2,128,1]{2,0,1:T(2,128)S(1)}, u32[]{:S(2)}, u32[]{:S(2)}) collective-permute-start(f32[2,128,1]{2,0,1:T(2,128)S(1)} %get-tuple-element.230), channel_id=1, source_target_pairs={{0,4},{4,8},{8,12},{12,16},{16,20},{20,24},{24,28},{1,5},{5,9},{9,... | collective-permute-start | bytes 3080 | tf_op jit(solution)/shard_map/ppermute | solution.py:16
  5.0 5.4 %collective-permute-start.1 = (f32[2,128,1]{2,0,1:T(2,128)S(1)}, f32[2,128,1]{2,0,1:T(2,128)S(1)}, u32[]{:S(2)}, u32[]{:S(2)}) collective-permute-start(f32[2,128,1]{2,0,1:T(2,128)S(1)} %get-tuple-element.231), channel_id=1, source_target_pairs={{4,0},{8,4},{12,8},{16,12},{20,16},{24,20},{28,24},{5,1},{9,5},{13... | collective-permute-start | bytes 3080 | tf_op jit(solution)/shard_map/ppermute | solution.py:19
  6.3 0.7 copy-start.3
  7.5 0.7 copy-start.4
  8.7 6.5 %copy-start.1 = (f32[2,128,128]{2,1,0:T(8,128)S(1)}, f32[2,128,128]{2,1,0:T(8,128)}, u32[]{:S(2)}) copy-start(f32[2,128,128]{2,1,0:T(8,128)} %param.6) | copy-start | bytes 393220
  10.5 5.5 %collective-permute-start.2 = (f32[2,1,130]{2,0,1:T(2,128)S(1)}, f32[2,1,130]{2,0,1:T(2,128)S(1)}, u32[]{:S(2)}, u32[]{:S(2)}) collective-permute-start(f32[2,1,130]{2,0,1:T(2,128)S(1)} %get-tuple-element.73), channel_id=1, source_target_pairs={{0,1},{1,2},{2,3},{4,5},{5,6},{6,7},{8,9},{9,10},{10,11},{12,13},{... | collective-permute-start | bytes 3128 | tf_op jit(solution)/shard_map/ppermute | solution.py:16
  13.9 5.5 %collective-permute-start.3 = (f32[2,1,130]{2,0,1:T(2,128)S(1)}, f32[2,1,130]{2,0,1:T(2,128)S(1)}, u32[]{:S(2)}, u32[]{:S(2)}) collective-permute-start(f32[2,1,130]{2,0,1:T(2,128)S(1)} %get-tuple-element.74), channel_id=1, source_target_pairs={{1,0},{2,1},{3,2},{5,4},{6,5},{7,6},{9,8},{10,9},{11,10},{13,12},{... | collective-permute-start | bytes 3128 | tf_op jit(solution)/shard_map/ppermute | solution.py:19
  19.4 0.7 copy-start.5
  22.5 8.8 %all-to-all-start.5 = ((f32[2,128,128]{1,0,2:T(2,128)}), f32[2,128,128]{1,0,2:T(2,128)S(1)}, u32[]{:S(2)}, u32[]{:S(2)}) async-start(f32[2,128,128]{1,0,2:T(2,128)} %copy.74), calls=%async_computation.5 | async-start | bytes 262144 | tf_op jit(solution)/shard_map/all_to_all | solution.py:111
  31.3 8.6 %all-to-all-start.6 = ((f32[2,128,128]{1,0,2:T(2,128)}), f32[2,128,128]{1,0,2:T(2,128)S(1)}, u32[]{:S(2)}, u32[]{:S(2)}) async-start(f32[2,128,128]{1,0,2:T(2,128)} %copy.77), calls=%async_computation.6 | async-start | bytes 262144 | tf_op jit(solution)/shard_map/all_to_all | solution.py:112
  39.9 13.0 %all-to-all-start = ((f32[2,128,128]{2,0,1:T(2,128)}), f32[2,128,128]{2,0,1:T(2,128)S(1)}, u32[]{:S(2)}, u32[]{:S(2)}) async-start(f32[2,128,128]{2,0,1:T(2,128)} %copy.61), calls=%async_computation | async-start | bytes 262144 | tf_op jit(solution)/shard_map/all_to_all | solution.py:105
  52.9 10.1 %all-to-all-start.1 = ((f32[2,128,128]{2,0,1:T(2,128)}), f32[2,128,128]{2,0,1:T(2,128)S(1)}, u32[]{:S(2)}, u32[]{:S(2)}) async-start(f32[2,128,128]{2,0,1:T(2,128)} %fusion.12), calls=%async_computation.1 | async-start | bytes 262144 | tf_op jit(solution)/shard_map/all_to_all | solution.py:106
  63.0 10.1 %all-to-all-start.2 = ((f32[2,128,128]{2,0,1:T(2,128)}), f32[2,128,128]{2,0,1:T(2,128)S(1)}, u32[]{:S(2)}, u32[]{:S(2)}) async-start(f32[2,128,128]{2,0,1:T(2,128)} %get-tuple-element.75), calls=%async_computation.2 | async-start | bytes 262144 | tf_op jit(solution)/shard_map/all_to_all | solution.py:107
  81.7 10.1 %all-to-all-start.3 = ((f32[8,1,4096]{2,1,0:T(1,128)}), f32[8,1,4096]{2,1,0:T(1,128)S(1)}, u32[]{:S(2)}, u32[]{:S(2)}) async-start(f32[8,1,4096]{2,1,0:T(1,128)} %reshape.78), calls=%async_computation.3 | async-start | bytes 262144 | tf_op jit(solution)/shard_map/all_to_all | solution.py:109
  94.9 0.8 copy-start
  95.7 8.3 %all-to-all-start.4 = ((f32[2,128,128]{1,0,2:T(2,128)}), f32[2,128,128]{1,0,2:T(2,128)S(1)}, u32[]{:S(2)}, u32[]{:S(2)}) async-start(f32[2,128,128]{1,0,2:T(2,128)} %copy.71), calls=%async_computation.4 | async-start | bytes 262144 | tf_op jit(solution)/shard_map/all_to_all | solution.py:110
where the time goes:
time: 121 us; the launch traced here: 120 us
  waiting for transfers between devices  45 us (37%)
  starting transfers between devices  35.2 us (29%)
  local copies, waits for them, and re-layouts  18.4 us (15%)
  other arithmetic  12.2 us (10%)
  blocking collectives  7.41 us (6%)
  between operations  1.82 us (2%)
    unnamed x19, local copies, waits for them, and re-layouts  8.12 us
    all_to_all x1, blocking collectives, per_device(): lax.all_to_all(solved, 'gy', split_axis=1, concat_axis=2, tiled=True)  7.41 us
    all_to_all x1, waiting for transfers between devices, per_device(): lax.all_to_all(fields, 'gx', split_axis=1, concat_axis=2, tiled=True)  6.72 us
    all_to_all x1, waiting for transfers between devices, per_device(): lax.all_to_all(solved, 'gx', split_axis=2, concat_axis=1, tiled=True)  6.61 us
    all_to_all x1, waiting for transfers between devices, per_device(): lax.all_to_all(east_face, 'gx', split_axis=1, concat_axis=2, tiled=True)  6.59 us
    all_to_all x1, waiting for transfers between devices, per_device(): lax.all_to_all(west_face, 'gx', split_axis=1, concat_axis=2, tiled=True)  6.49 us
    all_to_all x1, starting transfers between devices, per_device(): lax.all_to_all(fields, 'gx', split_axis=1, concat_axis=2, tiled=True)  6.23 us
    ppermute x2, starting transfers between devices, with_halo(): lax.ppermute(lax.slice_in_dim(block, block.shape[dim] - width, None, axis...  5.75 us
  transfers between devices with their start and end apart: 11, of which 9 were waited for; matrix products, arithmetic and copies ran while one was open for 3% of the time, Pallas kernels for 0%

commit v1 on v0

v1 whole, which is shorter than its diff:
```python
import functools

import jax
import jax.numpy as jnp
from jax import lax
from jax.experimental import pallas as pl
from jax.experimental.pallas import tpu as pltpu
from jax.sharding import PartitionSpec as P

MATERIALS = 8
FOURIER = 8192
DRYING = 4096
SCALES = (0.5 * FOURIER, 0.5 * DRYING)
SUB = 8
SLOT = 16
ROWS = 14


def lookup(conduct, comp, mats):
    low, mid, high = mats
    v = [conduct[comp, k] for k in range(MATERIALS)]
    pair = [jnp.where(low, v[2 * k + 1], v[2 * k]) for k in range(4)]
    quad = [jnp.where(mid, pair[2 * k + 1], pair[2 * k]) for k in range(2)]
    return jnp.where(high, quad[1], quad[0])


def fold(links, ground):
    ground = list(ground)
    index = list(range(len(ground)))
    plan = []
    while len(index) > 2:
        keep, merged = [index[0]], []
        p = 1
        while p < len(index):
            if p + 1 < len(index):
                a, k, b = index[p - 1 : p + 2]
                w = 1.0 / (links[p - 1] + links[p] + ground[k])
                lo, hi = links[p - 1] * w, links[p] * w
                merged.append(links[p - 1] * hi)
                ground[a] = ground[a] + lo * ground[k]
                ground[b] = ground[b] + hi * ground[k]
                plan.append((a, k, b, lo, hi, w))
                keep.append(b)
                p += 2
            else:
                merged.append(links[p - 1])
                keep.append(index[p])
                p += 1
        index, links = keep, merged
    return plan, links[0], ground[0], ground[-1]


def fold_source(plan, source):
    source = list(source)
    for a, k, b, lo, hi, _ in plan:
        source[a] = source[a] + lo * source[k]
        source[b] = source[b] + hi * source[k]
    return source


def unfold(plan, source, first, last):
    x = {0: first, len(source) - 1: last}
    for a, k, b, lo, hi, w in reversed(plan):
        x[k] = source[k] * w + lo * x[a] + hi * x[b]
    return [x[k] for k in range(len(source))]


def roll(x, shift):
    return pltpu.roll(x, shift % x.shape[0], 0)


def block_structure(conduct, mat_ref, joints, base):
    span = mat_ref.shape[0] // SUB
    lane = mat_ref.shape[1]
    sub = lax.broadcasted_iota(jnp.int32, (SUB, lane), 0)
    bits = jnp.zeros((SUB, lane), jnp.int32)
    for k in range(joints.shape[0]):
        at = joints[k : k + 1, :] - base - sub * span
        bits = bits | jnp.where(
            (at >= 1) & (at <= span), jnp.left_shift(1, jnp.clip(at, 0, span)), 0
        )
    masks = []
    for t in range(span):
        mat = mat_ref[pl.ds(t, SUB, stride=span), :]
        masks.append(((mat & 1) != 0, (mat & 2) != 0, (mat & 4) != 0))
    cut = [(bits & (1 << (t + 1))) != 0 for t in range(span)]
    out = []
    for comp in range(2):
        cond = [lookup(conduct, comp, m) for m in masks]
        after = cond[1:] + [roll(cond[0], -1)]
        face = [
            jnp.where(cut[t], 0.0, SCALES[comp] * (cond[t] + after[t])) for t in range(span)
        ]
        ones = jnp.ones((SUB, lane), jnp.float32)
        plan, b, gp, gq = fold(face[:-1], [ones] * span)
        link = jnp.where(sub == SUB - 1, 0.0, face[-1])
        wq = 1.0 / (b + link + gq)
        lo = jnp.where(sub == SUB - 1, 0.0, b * wq)
        hi = link * wq
        c = jnp.where(sub == SUB - 1, b, b * hi)
        a = jnp.where(sub == 0, 0.0, roll(c, 1))
        g = gp + lo * gq + roll(hi * gq, 1)
        g_first = g
        steps = []
        s = 1
        while s < SUB:
            w = 1.0 / (a + c + g)
            right = jnp.where((sub >= 1) & (sub <= SUB - 1 - s), c * w, 0.0)
            left = jnp.where(sub >= 1 + s, a * w, 0.0)
            steps.append((s, right, left))
            g_new = g + roll(right * g, s) + roll(left * g, -s)
            a_new = jnp.where(sub >= 1 + s, roll(right * a, s), a)
            c_new = jnp.where(sub <= SUB - 1 - s, roll(left * c, -s), c)
            a, c, g = a_new, c_new, g_new
            s *= 2
        w = 1.0 / (a + c + g)
        aw, cw = a * w, c * w
        between = (aw * c)[1:2, :]
        ground0 = g_first[0:1, :] + (aw * g)[1:2, :]
        ground1 = (gq + cw * g)[SUB - 1 : SUB, :]
        cond0 = cond[0][0:1, :]
        cond1 = cond[-1][SUB - 1 : SUB, :]
        inner = dict(
            plan=plan, b=b, link=link, wq=wq, lo=lo, hi=hi, steps=steps, w=w, aw=aw, cw=cw
        )
        out.append((inner, (between, ground0, ground1, cond0, cond1)))
    return out


def block_source(inner, source):
    source = fold_source(inner["plan"], source)
    fq = source[-1]
    f = source[0] + inner["lo"] * fq + roll(inner["hi"] * fq, 1)
    f_first = f
    for s, right, left in inner["steps"]:
        f = f + roll(right * f, s) + roll(left * f, -s)
    f0 = f_first[0:1, :] + (inner["aw"] * f)[1:2, :]
    f1 = (fq + inner["cw"] * f)[SUB - 1 : SUB, :]
    return (source, f), f0, f1


def block_solve(inner, kept, first, last):
    source, f = kept
    sub = lax.broadcasted_iota(jnp.int32, f.shape, 0)
    xp = f * inner["w"] + inner["aw"] * first + inner["cw"] * last
    xp = jnp.where(sub == 0, first, xp)
    xq = (source[-1] + inner["b"] * xp + inner["link"] * roll(xp, -1)) * inner["wq"]
    xq = jnp.where(sub == SUB - 1, last, xq)
    return unfold(inner["plan"], source, xp, xq)


def chain_solve(comp, held, joints, count, block):
    slots = held.shape[0] // SLOT

    def item(q):
        return held[pl.ds(7 * comp + q, slots, stride=SLOT), :]

    b, g0, g1, k0, k1, f0, f1 = [item(q) for q in range(7)]
    pos = lax.broadcasted_iota(jnp.int32, b.shape, 0)
    cut = pos >= count - 1
    for k in range(joints.shape[0]):
        cut = cut | (joints[k : k + 1, :] == (pos + 1) * block)
    link = jnp.where(cut, 0.0, SCALES[comp] * (k1 + roll(k0, -1)))
    wr = 1.0 / (b + link + g1)
    lo, hi = b * wr, link * wr
    c = b * hi
    a = roll(c, 1)
    g = g0 + lo * g1 + roll(hi * g1, 1)
    f = f0 + lo * f1 + roll(hi * f1, 1)
    s = 1
    while s < count:
        w = 1.0 / (a + c + g)
        right, left = c * w, a * w
        f = f + roll(right * f, s) + roll(left * f, -s)
        g_new = g + roll(right * g, s) + roll(left * g, -s)
        a, c, g = roll(right * a, s), roll(left * c, -s), g_new
        s *= 2
    x0 = f / g
    x1 = (f1 + b * x0 + link * roll(x0, -1)) * wr
    return x0, x1


def kernel(
    fields, material, conduct, joints_x, joints_y, half, advanced,
    field_t, mat_t, half_t, held_x, held_y, ends,
    send_x, recv_x, send_y, recv_y,
):
    nx, ny = lax.axis_size("gx"), lax.axis_size("gy")
    mx, my = lax.axis_index("gx"), lax.axis_index("gy")
    rows, cols = material.shape
    axes = (("gx", nx, mx, held_x, send_x, recv_x), ("gy", ny, my, held_y, send_y, recv_y))

    barrier = pltpu.get_barrier_semaphore()
    for axis, n, me, _, _, _ in axes:
        for off in range(1, n):
            pl.semaphore_signal(
                barrier, inc=1, device_id={axis: lax.rem(me + off, n)},
                device_id_type=pl.DeviceIdType.MESH,
            )

    for axis, n, me, held, _, _ in axes:
        slots = held.shape[0] // SLOT
        if slots > n:
            held[n * SLOT :, :] = jnp.ones(((slots - n) * SLOT, cols), jnp.float32)

    def copy_to(which, off):
        axis, n, me, held, send, recv = axes[which]
        peer = lax.rem(me + off, n)
        own = held.at[pl.ds(pl.multiple_of(me * SLOT, SLOT), SLOT), :]
        return pltpu.make_async_remote_copy(
            src_ref=own, dst_ref=own, send_sem=send.at[off], recv_sem=recv.at[me],
            device_id={axis: peer}, device_id_type=pl.DeviceIdType.MESH,
        )

    def copy_from(which, off):
        axis, n, me, held, send, recv = axes[which]
        peer = lax.rem(me + off, n)
        theirs = held.at[pl.ds(pl.multiple_of(peer * SLOT, SLOT), SLOT), :]
        return pltpu.make_async_remote_copy(
            src_ref=theirs, dst_ref=theirs, send_sem=send.at[off], recv_sem=recv.at[peer],
            device_id={axis: peer}, device_id_type=pl.DeviceIdType.MESH,
        )

    def publish(which, parts):
        _, n, me, held, _, _ = axes[which]
        lines = [row for part in parts for row in part]
        lines += [jnp.zeros_like(lines[0])] * (SLOT - len(lines))
        held[pl.ds(pl.multiple_of(me * SLOT, SLOT), SLOT), :] = jnp.concatenate(lines, axis=0)

    def gather_ends(which, joints, block):
        _, n, me, held, _, _ = axes[which]
        slots = held.shape[0] // SLOT
        found = []
        for comp in range(2):
            x0, x1 = chain_solve(comp, held, joints, n, block)
            ends[pl.ds(0, slots), :] = x0
            ends[pl.ds(slots, slots), :] = x1
            found.append((ends[pl.ds(me, 1), :], ends[pl.ds(me + slots, 1), :]))
        return found

    mat_t[...] = material[...].T
    for comp in range(2):
        field_t[comp] = fields[comp].T
    jx, jy = joints_x[...], joints_y[...]

    span = cols // SUB
    along_x = block_structure(conduct, mat_t, jx, mx * cols)
    kept_x, parts = [], []
    for comp in range(2):
        inner, shared = along_x[comp]
        kept, f0, f1 = block_source(
            inner, [field_t[comp, pl.ds(t, SUB, stride=span), :] for t in range(span)]
        )
        kept_x.append(kept)
        parts.append(shared + (f0, f1))
    publish(0, parts)
    pl.semaphore_wait(barrier, nx + ny - 2)
    for off in range(1, nx):
        copy_to(0, off).start()
    span_y = rows // SUB
    along_y = block_structure(conduct, material, jy, my * rows)
    for off in range(1, nx):
        copy_from(0, off).wait_recv()
    found = gather_ends(0, jx, cols)
    for comp in range(2):
        x = block_solve(along_x[comp][0], kept_x[comp], *found[comp])
        for t in range(span):
            half_t[comp, pl.ds(t, SUB, stride=span), :] = x[t]
        half[comp] = half_t[comp].T

    kept_y, parts = [], []
    for comp in range(2):
        inner, shared = along_y[comp]
        kept, f0, f1 = block_source(
            inner, [half[comp, pl.ds(t, SUB, stride=span_y), :] for t in range(span_y)]
        )
        kept_y.append(kept)
        parts.append(shared + (f0, f1))
    publish(1, parts)
    for off in range(1, ny):
        copy_to(1, off).start()
    for off in range(1, ny):
        copy_from(1, off).wait_recv()
    found = gather_ends(1, jy, rows)
    for comp in range(2):
        x = block_solve(along_y[comp][0], kept_y[comp], *found[comp])
        for t in range(span_y):
            advanced[comp, pl.ds(t, SUB, stride=span_y), :] = x[t]
    for off in range(1, nx):
        copy_to(0, off).wait_send()
    for off in range(1, ny):
        copy_to(1, off).wait_send()


def per_device(nx, ny, fields, material, conduct, joints_x, joints_y):
    rows, cols = material.shape
    vmem = pl.BlockSpec(memory_space=pltpu.VMEM)
    shape = jax.ShapeDtypeStruct(fields.shape, jnp.float32)
    sx, sy = max(nx, SUB), max(ny, SUB)
    return pl.pallas_call(
        kernel,
        out_shape=(shape, shape),
        in_specs=[vmem, vmem, pl.BlockSpec(memory_space=pltpu.SMEM), vmem, vmem],
        out_specs=(vmem, vmem),
        scratch_shapes=[
            pltpu.VMEM((2, cols, rows), jnp.float32),
            pltpu.VMEM((cols, rows), jnp.int32),
            pltpu.VMEM((2, cols, rows), jnp.float32),
            pltpu.VMEM((sx * SLOT, rows), jnp.float32),
            pltpu.VMEM((sy * SLOT, cols), jnp.float32),
            pltpu.VMEM((2 * max(sx, sy), cols), jnp.float32),
            pltpu.SemaphoreType.DMA((nx,)),
            pltpu.SemaphoreType.DMA((nx,)),
            pltpu.SemaphoreType.DMA((ny,)),
            pltpu.SemaphoreType.DMA((ny,)),
        ],
        compiler_params=pltpu.CompilerParams(
            collective_id=0, has_side_effects=True, vmem_limit_bytes=16 * 1024 * 1024
        ),
    )(fields, material, conduct, joints_x.T, joints_y.T)


def solution(mesh):
    return jax.shard_map(
        functools.partial(per_device, mesh.shape["gx"], mesh.shape["gy"]),
        mesh=mesh,
        in_specs=(P(None, "gy", "gx"), P("gy", "gx"), P(), P("gy", None), P("gx", None)),
        out_specs=(P(None, "gy", "gx"), P(None, "gy", "gx")),
        check_vma=False,
    )
```

time: 121 us -> 18.9 us (0.16)
  waiting for transfers between devices: 45 us -> 0 us
  starting transfers between devices: 35.2 us -> 0 us
  local copies, waits for them, and re-layouts: 18.4 us -> 5.1 us
  Pallas kernels: 0 us -> 12.9 us
  other arithmetic: 12.2 us -> 0 us
  blocking collectives: 7.41 us -> 0 us
    all_to_all x7 -> x0, waiting for transfers between devices: 39.9 us -> none  [the longest x1 6.72 us: per_device(): lax.all_to_all(fields, 'gx', split_axis=1, concat_axis=2, tiled=True)]
    all_to_all x7 -> x0, starting transfers between devices: 26.8 us -> none  [the longest x1 6.23 us: per_device(): lax.all_to_all(fields, 'gx', split_axis=1, concat_axis=2, tiled=True)]
    pallas_call x0 -> x1, Pallas kernels: none -> 12.9 us  [per_device(): pl.pallas_call(kernel, out_shape=(shape, shape), in_specs=[vmem, vmem, pl...]
    ppermute x4 -> x0, starting transfers between devices: 8.33 us -> none  [the longest x2 5.75 us: with_halo(): lax.ppermute(lax.slice_in_dim(block, block.shape[dim] - width, None, axis...]
    all_to_all x1 -> x0, blocking collectives: 7.41 us -> none  [per_device(): lax.all_to_all(solved, 'gy', split_axis=1, concat_axis=2, tiled=True)]
    slice x78 -> x0, local copies, waits for them, and re-layouts: 5.97 us -> none  [the longest x38 2.75 us: shifted(): lax.slice_in_dim(array_in, stride, length, axis=line_axis)]
    ppermute x4 -> x0, waiting for transfers between devices: 5.09 us -> none  [the longest x2 5.09 us: with_halo(): lax.ppermute(lax.slice_in_dim(block, 0, width, axis=dim), axis, backward)]
    add x32 -> x0, other arithmetic: 5.03 us -> none  [the longest x15 2.9 us: cyclic(): entry + before_gain * shifted(entry, stride, line_axis, 0.0, True)]
  transfers between devices with their start and end apart: 11 -> 0, of which waited for: 9 -> 0; matrix products, arithmetic and copies ran while one was open for 3% -> 0% of each run, Pallas kernels for 0% -> 0%
where the time goes in v1:
time: 18.9 us; the launch traced here: 18.7 us
  Pallas kernels  12.9 us (68%)
  local copies, waits for them, and re-layouts  5.1 us (27%)
  between operations  0.65 us (3%)
    pallas_call x1, Pallas kernels, per_device(): pl.pallas_call(kernel, out_shape=(shape, shape), in_specs=[vmem, vmem, pl...  12.9 us
    unnamed x12, local copies, waits for them, and re-layouts  5.1 us

profile of v1, /device:TPU:0, one launch (start us, length us, event | category | flops | bytes accessed | tf_op | source)
XLA Modules:
  0.0 18.7 jit_solution(1324994385837680346)
XLA Ops:
  0.6 0.0 copy-start.4
  0.6 0.7 %copy-done.4 = f32[2,8]{1,0:T(2,128)S(1)} copy-done((f32[2,8]{1,0:T(2,128)S(1)}, f32[2,8]{1,0:T(2,128)}, u32[]{:S(2)}) %copy-start.4) | copy-done | bytes 88
  1.3 0.0 copy-start
  1.3 0.9 %copy-done = f32[2,128,128]{2,1,0:T(8,128)S(1)} copy-done((f32[2,128,128]{2,1,0:T(8,128)S(1)}, f32[2,128,128]{2,1,0:T(8,128)}, u32[]{:S(2)}) %copy-start) | copy-done | bytes 131096
  2.2 0.0 copy-start.1
  2.2 0.8 %copy-done.1 = s32[128,128]{1,0:T(8,128)S(1)} copy-done((s32[128,128]{1,0:T(8,128)S(1)}, s32[128,128]{1,0:T(8,128)}, u32[]{:S(2)}) %copy-start.1) | copy-done | bytes 65560
  3.1 0.0 copy-start.2
  3.1 0.7 %copy-done.2 = s32[128,8]{0,1:T(8,128)S(1)} copy-done((s32[128,8]{0,1:T(8,128)S(1)}, s32[128,8]{0,1:T(8,128)}, u32[]{:S(2)}) %copy-start.2) | copy-done | bytes 4120
  3.7 0.0 copy-start.3
  3.7 0.7 %copy-done.3 = s32[128,8]{0,1:T(8,128)S(1)} copy-done((s32[128,8]{0,1:T(8,128)S(1)}, s32[128,8]{0,1:T(8,128)}, u32[]{:S(2)}) %copy-start.3) | copy-done | bytes 4120
  4.4 12.9 %shard_map.68 = (f32[2,128,128]{2,1,0:T(8,128)S(1)}, f32[2,128,128]{2,1,0:T(8,128)S(1)}) custom-call(f32[2,128,128]{2,1,0:T(8,128)S(1)} %copy-done, s32[128,128]{1,0:T(8,128)S(1)} %copy-done.1, f32[2,8]{1,0:T(2,128)S(1)} %copy-done.4, s32[8,128]{1,0:T(8,128)S(1)} %bitcast.2, s32[8,128]{1,0:T(8,128)S(1)} %bitcast.3), custom_call_target="tpu_custom_call" | custom-call | tf_op jit(solution)/shard_map/pallas_call | solution.py:300
  17.4 0.7 %copy.9 = f32[2,128,128]{2,1,0:T(8,128)} copy(f32[2,128,128]{2,1,0:T(8,128)S(1)} %get-tuple-element.4) | data formatting | bytes 262144
  18.0 0.7 %copy.10 = f32[2,128,128]{2,1,0:T(8,128)} copy(f32[2,128,128]{2,1,0:T(8,128)S(1)} %get-tuple-element.5) | data formatting | bytes 262144
Async XLA Ops:
  0.6 0.7 %copy-start.4 = (f32[2,8]{1,0:T(2,128)S(1)}, f32[2,8]{1,0:T(2,128)}, u32[]{:S(2)}) copy-start(f32[2,8]{1,0:T(2,128)} %conduct.1) | copy-start | bytes 196
  1.3 0.9 %copy-start = (f32[2,128,128]{2,1,0:T(8,128)S(1)}, f32[2,128,128]{2,1,0:T(8,128)}, u32[]{:S(2)}) copy-start(f32[2,128,128]{2,1,0:T(8,128)} %fields.1) | copy-start | bytes 393220
  2.2 0.8 %copy-start.1 = (s32[128,128]{1,0:T(8,128)S(1)}, s32[128,128]{1,0:T(8,128)}, u32[]{:S(2)}) copy-start(s32[128,128]{1,0:T(8,128)} %material.1) | copy-start | bytes 196612
  3.1 0.7 %copy-start.2 = (s32[128,8]{0,1:T(8,128)S(1)}, s32[128,8]{0,1:T(8,128)}, u32[]{:S(2)}) copy-start(s32[128,8]{0,1:T(8,128)} %param.8) | copy-start | bytes 12292
  3.7 0.7 %copy-start.3 = (s32[128,8]{0,1:T(8,128)S(1)}, s32[128,8]{0,1:T(8,128)}, u32[]{:S(2)}) copy-start(s32[128,8]{0,1:T(8,128)} %param.9) | copy-start | bytes 12292

commit v2 on v1

--- a/solution.py
+++ b/solution.py
@@ -181,9 +181,10 @@
 
 
 def kernel(
-    fields, material, conduct, joints_x, joints_y, half, advanced,
+    fields_in, material_in, conduct_in, joints_x_in, joints_y_in, half, advanced,
+    fields, material, conduct, joints_x, joints_y,
     field_t, mat_t, half_t, held_x, held_y, ends,
-    send_x, recv_x, send_y, recv_y,
+    send_x, recv_x, send_y, recv_y, load_sem,
 ):
     nx, ny = lax.axis_size("gx"), lax.axis_size("gy")
     mx, my = lax.axis_index("gx"), lax.axis_index("gy")
@@ -197,6 +198,21 @@
                 barrier, inc=1, device_id={axis: lax.rem(me + off, n)},
                 device_id_type=pl.DeviceIdType.MESH,
             )
+
+    loads = [
+        pltpu.make_async_copy(source, target, load_sem.at[i])
+        for i, (source, target) in enumerate(
+            (
+                (material_in, material),
+                (conduct_in, conduct),
+                (joints_x_in, joints_x),
+                (fields_in, fields),
+                (joints_y_in, joints_y),
+            )
+        )
+    ]
+    for load in loads:
+        load.start()
 
     for axis, n, me, held, _, _ in axes:
         slots = held.shape[0] // SLOT
@@ -238,10 +254,12 @@
             found.append((ends[pl.ds(me, 1), :], ends[pl.ds(me + slots, 1), :]))
         return found
 
+    for load in loads[:4]:
+        load.wait()
     mat_t[...] = material[...].T
     for comp in range(2):
         field_t[comp] = fields[comp].T
-    jx, jy = joints_x[...], joints_y[...]
+    jx = joints_x[...]
 
     span = cols // SUB
     along_x = block_structure(conduct, mat_t, jx, mx * cols)
@@ -257,6 +275,8 @@
     pl.semaphore_wait(barrier, nx + ny - 2)
     for off in range(1, nx):
         copy_to(0, off).start()
+    loads[4].wait()
+    jy = joints_y[...]
     span_y = rows // SUB
     along_y = block_structure(conduct, material, jy, my * rows)
     for off in range(1, nx):
@@ -292,17 +312,35 @@
         copy_to(1, off).wait_send()
 
 
+def write_out(half, advanced, half_out, advanced_out, sems):
+    copies = [
+        pltpu.make_async_copy(half, half_out, sems.at[0]),
+        pltpu.make_async_copy(advanced, advanced_out, sems.at[1]),
+    ]
+    for copy in copies:
+        copy.start()
+    for copy in copies:
+        copy.wait()
+
+
 def per_device(nx, ny, fields, material, conduct, joints_x, joints_y):
     rows, cols = material.shape
+    joints = joints_x.shape[1]
     vmem = pl.BlockSpec(memory_space=pltpu.VMEM)
+    hbm = pl.BlockSpec(memory_space=pltpu.HBM)
     shape = jax.ShapeDtypeStruct(fields.shape, jnp.float32)
     sx, sy = max(nx, SUB), max(ny, SUB)
-    return pl.pallas_call(
+    solved = pl.pallas_call(
         kernel,
         out_shape=(shape, shape),
-        in_specs=[vmem, vmem, pl.BlockSpec(memory_space=pltpu.SMEM), vmem, vmem],
+        in_specs=[hbm] * 5,
         out_specs=(vmem, vmem),
         scratch_shapes=[
+            pltpu.VMEM((2, rows, cols), jnp.float32),
+            pltpu.VMEM((rows, cols), jnp.int32),
+            pltpu.SMEM(conduct.shape, jnp.float32),
+            pltpu.VMEM((joints, rows), jnp.int32),
+            pltpu.VMEM((joints, cols), jnp.int32),
             pltpu.VMEM((2, cols, rows), jnp.float32),
             pltpu.VMEM((cols, rows), jnp.int32),
             pltpu.VMEM((2, cols, rows), jnp.float32),
@@ -313,11 +351,25 @@
             pltpu.SemaphoreType.DMA((nx,)),
             pltpu.SemaphoreType.DMA((ny,)),
             pltpu.SemaphoreType.DMA((ny,)),
+            pltpu.SemaphoreType.DMA((5,)),
         ],
         compiler_params=pltpu.CompilerParams(
             collective_id=0, has_side_effects=True, vmem_limit_bytes=16 * 1024 * 1024
         ),
-    )(fields, material, conduct, joints_x.T, joints_y.T)
+    )(
+        *(
+            pltpu.with_memory_space_constraint(x, pltpu.HBM)
+            for x in (fields, material, conduct, joints_x.T, joints_y.T)
+        )
+    )
+    return pl.pallas_call(
+        write_out,
+        out_shape=(shape, shape),
+        in_specs=[vmem, vmem],
+        out_specs=(hbm, hbm),
+        scratch_shapes=[pltpu.SemaphoreType.DMA((2,))],
+        compiler_params=pltpu.CompilerParams(vmem_limit_bytes=4 * 1024 * 1024),
+    )(*solved)
 
 
 def solution(mesh):

time: 18.9 us -> 14.4 us (0.76)
  local copies, waits for them, and re-layouts: 5.1 us -> 0 us
  Pallas kernels: 12.9 us -> 13.6 us
    unnamed x12 -> x0, local copies, waits for them, and re-layouts: 5.1 us -> none
    pallas_call x1 -> x2, Pallas kernels: 12.9 us -> 13.6 us  [the longest x1 12.9 us: per_device(): pl.pallas_call(kernel, out_shape=(shape, shape), in_specs=[hbm] * 5, out_...]
where the time goes in v2:
time: 14.4 us; the launch traced here: 14.2 us
  Pallas kernels  13.6 us (94%)
  between operations  0.64 us (4%)
    pallas_call x1, Pallas kernels, per_device(): pl.pallas_call(kernel, out_shape=(shape, shape), in_specs=[hbm] * 5, out_...  12.9 us
    pallas_call x1, Pallas kernels, per_device(): pl.pallas_call(write_out, out_shape=(shape, shape), in_specs=[vmem, vmem]...  0.72 us

profile of v2, /device:TPU:0, one launch (start us, length us, event | category | flops | bytes accessed | tf_op | source)
XLA Modules:
  0.0 14.2 jit_solution(10768487524101169715)
XLA Ops:
  0.6 12.9 %shard_map.68 = (f32[2,128,128]{2,1,0:T(8,128)S(1)}, f32[2,128,128]{2,1,0:T(8,128)S(1)}) custom-call(f32[2,128,128]{2,1,0:T(8,128)} %fields_in.1, s32[128,128]{1,0:T(8,128)} %material_in.1, f32[2,8]{1,0:T(2,128)} %conduct_in.1, s32[8,128]{1,0:T(8,128)} %bitcast.2, s32[8,128]{1,0:T(8,128)} %bitcast.3), custom_call_target="tpu_custom_call" | custom-call | tf_op jit(solution)/shard_map/pallas_call | solution.py:333
  13.5 0.7 %shard_map.69 = (f32[2,128,128]{2,1,0:T(8,128)}, f32[2,128,128]{2,1,0:T(8,128)}) custom-call(f32[2,128,128]{2,1,0:T(8,128)S(1)} %get-tuple-element.4.half, f32[2,128,128]{2,1,0:T(8,128)S(1)} %get-tuple-element.5.advanced), custom_call_target="tpu_custom_call" | custom-call | tf_op jit(solution)/shard_map/pallas_call | solution.py:365

commit v3 on v2

--- a/solution.py
+++ b/solution.py
@@ -13,7 +13,12 @@
 SCALES = (0.5 * FOURIER, 0.5 * DRYING)
 SUB = 8
 SLOT = 16
-ROWS = 14
+ROWS = 12
+
+
+def inverse(x):
+    guess = pl.reciprocal(x, approx=True)
+    return guess * (2.0 - x * guess)
 
 
 def lookup(conduct, comp, mats):
@@ -22,6 +27,10 @@
     pair = [jnp.where(low, v[2 * k + 1], v[2 * k]) for k in range(4)]
     quad = [jnp.where(mid, pair[2 * k + 1], pair[2 * k]) for k in range(2)]
     return jnp.where(high, quad[1], quad[0])
+
+
+def bit_masks(mat):
+    return (mat & 1) != 0, (mat & 2) != 0, (mat & 4) != 0
 
 
 def fold(links, ground):
@@ -34,7 +43,7 @@
         while p < len(index):
             if p + 1 < len(index):
                 a, k, b = index[p - 1 : p + 2]
-                w = 1.0 / (links[p - 1] + links[p] + ground[k])
+                w = inverse(links[p - 1] + links[p] + ground[k])
                 lo, hi = links[p - 1] * w, links[p] * w
                 merged.append(links[p - 1] * hi)
                 ground[a] = ground[a] + lo * ground[k]
@@ -81,8 +90,9 @@
         )
     masks = []
     for t in range(span):
-        mat = mat_ref[pl.ds(t, SUB, stride=span), :]
-        masks.append(((mat & 1) != 0, (mat & 2) != 0, (mat & 4) != 0))
+        last = mat_ref[pl.ds(t, SUB, stride=span), :]
+        first = last if t == 0 else first
+        masks.append(bit_masks(last))
     cut = [(bits & (1 << (t + 1))) != 0 for t in range(span)]
     out = []
     for comp in range(2):
@@ -94,7 +104,7 @@
         ones = jnp.ones((SUB, lane), jnp.float32)
         plan, b, gp, gq = fold(face[:-1], [ones] * span)
         link = jnp.where(sub == SUB - 1, 0.0, face[-1])
-        wq = 1.0 / (b + link + gq)
+        wq = inverse(b + link + gq)
         lo = jnp.where(sub == SUB - 1, 0.0, b * wq)
         hi = link * wq
         c = jnp.where(sub == SUB - 1, b, b * hi)
@@ -104,7 +114,7 @@
         steps = []
         s = 1
         while s < SUB:
-            w = 1.0 / (a + c + g)
+            w = inverse(a + c + g)
             right = jnp.where((sub >= 1) & (sub <= SUB - 1 - s), c * w, 0.0)
             left = jnp.where(sub >= 1 + s, a * w, 0.0)
             steps.append((s, right, left))
@@ -113,18 +123,16 @@
             c_new = jnp.where(sub <= SUB - 1 - s, roll(left * c, -s), c)
             a, c, g = a_new, c_new, g_new
             s *= 2
-        w = 1.0 / (a + c + g)
+        w = inverse(a + c + g)
         aw, cw = a * w, c * w
         between = (aw * c)[1:2, :]
         ground0 = g_first[0:1, :] + (aw * g)[1:2, :]
         ground1 = (gq + cw * g)[SUB - 1 : SUB, :]
-        cond0 = cond[0][0:1, :]
-        cond1 = cond[-1][SUB - 1 : SUB, :]
         inner = dict(
             plan=plan, b=b, link=link, wq=wq, lo=lo, hi=hi, steps=steps, w=w, aw=aw, cw=cw
         )
-        out.append((inner, (between, ground0, ground1, cond0, cond1)))
-    return out
+        out.append((inner, (between, ground0, ground1)))
+    return out, (first[0:1, :].astype(jnp.float32), last[SUB - 1 : SUB, :].astype(jnp.float32))
 
 
 def block_source(inner, source):
@@ -149,56 +157,58 @@
     return unfold(inner["plan"], source, xp, xq)
 
 
-def chain_solve(comp, held, joints, count, block):
-    slots = held.shape[0] // SLOT
-
-    def item(q):
-        return held[pl.ds(7 * comp + q, slots, stride=SLOT), :]
-
-    b, g0, g1, k0, k1, f0, f1 = [item(q) for q in range(7)]
+def chain_structure(conduct, comp, rows, mats, joints, count, block):
+    b, g0, g1 = rows
+    slots = b.shape[0]
     pos = lax.broadcasted_iota(jnp.int32, b.shape, 0)
     cut = pos >= count - 1
     for k in range(joints.shape[0]):
         cut = cut | (joints[k : k + 1, :] == (pos + 1) * block)
+    k0, k1 = [lookup(conduct, comp, bit_masks(m.astype(jnp.int32))) for m in mats]
     link = jnp.where(cut, 0.0, SCALES[comp] * (k1 + roll(k0, -1)))
-    wr = 1.0 / (b + link + g1)
+    wr = inverse(b + link + g1)
     lo, hi = b * wr, link * wr
     c = b * hi
     a = roll(c, 1)
     g = g0 + lo * g1 + roll(hi * g1, 1)
-    f = f0 + lo * f1 + roll(hi * f1, 1)
+    steps = []
     s = 1
     while s < count:
-        w = 1.0 / (a + c + g)
+        w = inverse(a + c + g)
         right, left = c * w, a * w
-        f = f + roll(right * f, s) + roll(left * f, -s)
+        steps.append((s, right, left))
         g_new = g + roll(right * g, s) + roll(left * g, -s)
         a, c, g = roll(right * a, s), roll(left * c, -s), g_new
         s *= 2
-    x0 = f / g
+    return b, link, wr, lo, hi, steps, inverse(g)
+
+
+def chain_source(structure, f0, f1):
+    b, link, wr, lo, hi, steps, w = structure
+    f = f0 + lo * f1 + roll(hi * f1, 1)
+    for s, right, left in steps:
+        f = f + roll(right * f, s) + roll(left * f, -s)
+    x0 = f * w
     x1 = (f1 + b * x0 + link * roll(x0, -1)) * wr
     return x0, x1
+
+
+def far_first(me, n, k):
+    down = n - 1 - k - lax.div(me + k + 1, n)
+    up = k + lax.div(k - me + n, n)
+    half = lax.div(2 * me, n)
+    return half * up + (1 - half) * down
 
 
 def kernel(
     fields_in, material_in, conduct_in, joints_x_in, joints_y_in, half, advanced,
     fields, material, conduct, joints_x, joints_y,
-    field_t, mat_t, half_t, held_x, held_y, ends,
-    send_x, recv_x, send_y, recv_y, load_sem,
+    field_t, mat_t, half_t, held_x, held_y, flow_y, ends,
+    send_x, recv_x, send_y, recv_y, send_f, recv_f, load_sem,
 ):
     nx, ny = lax.axis_size("gx"), lax.axis_size("gy")
     mx, my = lax.axis_index("gx"), lax.axis_index("gy")
     rows, cols = material.shape
-    axes = (("gx", nx, mx, held_x, send_x, recv_x), ("gy", ny, my, held_y, send_y, recv_y))
-
-    barrier = pltpu.get_barrier_semaphore()
-    for axis, n, me, _, _, _ in axes:
-        for off in range(1, n):
-            pl.semaphore_signal(
-                barrier, inc=1, device_id={axis: lax.rem(me + off, n)},
-                device_id_type=pl.DeviceIdType.MESH,
-            )
-
     loads = [
         pltpu.make_async_copy(source, target, load_sem.at[i])
         for i, (source, target) in enumerate(
@@ -214,102 +224,133 @@
     for load in loads:
         load.start()
 
-    for axis, n, me, held, _, _ in axes:
-        slots = held.shape[0] // SLOT
-        if slots > n:
-            held[n * SLOT :, :] = jnp.ones(((slots - n) * SLOT, cols), jnp.float32)
-
-    def copy_to(which, off):
-        axis, n, me, held, send, recv = axes[which]
-        peer = lax.rem(me + off, n)
-        own = held.at[pl.ds(pl.multiple_of(me * SLOT, SLOT), SLOT), :]
-        return pltpu.make_async_remote_copy(
-            src_ref=own, dst_ref=own, send_sem=send.at[off], recv_sem=recv.at[me],
-            device_id={axis: peer}, device_id_type=pl.DeviceIdType.MESH,
-        )
-
-    def copy_from(which, off):
-        axis, n, me, held, send, recv = axes[which]
-        peer = lax.rem(me + off, n)
-        theirs = held.at[pl.ds(pl.multiple_of(peer * SLOT, SLOT), SLOT), :]
-        return pltpu.make_async_remote_copy(
-            src_ref=theirs, dst_ref=theirs, send_sem=send.at[off], recv_sem=recv.at[peer],
-            device_id={axis: peer}, device_id_type=pl.DeviceIdType.MESH,
-        )
-
-    def publish(which, parts):
-        _, n, me, held, _, _ = axes[which]
-        lines = [row for part in parts for row in part]
-        lines += [jnp.zeros_like(lines[0])] * (SLOT - len(lines))
-        held[pl.ds(pl.multiple_of(me * SLOT, SLOT), SLOT), :] = jnp.concatenate(lines, axis=0)
-
-    def gather_ends(which, joints, block):
-        _, n, me, held, _, _ = axes[which]
-        slots = held.shape[0] // SLOT
-        found = []
-        for comp in range(2):
-            x0, x1 = chain_solve(comp, held, joints, n, block)
-            ends[pl.ds(0, slots), :] = x0
-            ends[pl.ds(slots, slots), :] = x1
-            found.append((ends[pl.ds(me, 1), :], ends[pl.ds(me + slots, 1), :]))
-        return found
-
-    for load in loads[:4]:
+    barrier = pltpu.get_barrier_semaphore()
+    peers_x = [far_first(mx, nx, k) for k in range(nx - 1)]
+    peers_y = [lax.rem(my + k, ny) for k in range(1, ny)]
+    for axis, peers in (("gx", peers_x), ("gy", peers_y)):
+        for peer in peers:
+            pl.semaphore_signal(
+                barrier, inc=1, device_id={axis: peer}, device_id_type=pl.DeviceIdType.MESH
+            )
+
+    class Exchange:
+        def __init__(self, axis, me, peers, held, slot, used, send, recv):
+            self.axis, self.me, self.peers, self.held = axis, me, peers, held
+            self.slot, self.used, self.send, self.recv = slot, used, send, recv
+            self.slots = held.shape[0] // slot
+            spare = self.slots - len(peers) - 1
+            if spare > 0:
+                held[(len(peers) + 1) * slot :, :] = jnp.ones(
+                    (spare * slot, held.shape[1]), jnp.float32
+                )
+
+        def copy(self, k, owner):
+            place = pl.multiple_of(owner * self.slot, self.slot)
+            block = self.held.at[pl.ds(place, self.used), :]
+            return pltpu.make_async_remote_copy(
+                src_ref=block, dst_ref=block, send_sem=self.send.at[k],
+                recv_sem=self.recv.at[owner], device_id={self.axis: self.peers[k]},
+                device_id_type=pl.DeviceIdType.MESH,
+            )
+
+        def publish(self, lines):
+            lines = list(lines) + [jnp.zeros_like(lines[0])] * (self.slot - len(lines))
+            place = pl.multiple_of(self.me * self.slot, self.slot)
+            self.held[pl.ds(place, self.slot), :] = jnp.concatenate(lines, axis=0)
+
+        def start(self):
+            for k in range(len(self.peers)):
+                self.copy(k, self.me).start()
+
+        def wait(self):
+            for k, peer in enumerate(self.peers):
+                self.copy(k, peer).wait_recv()
+
+        def finish(self):
+            for k in range(len(self.peers)):
+                self.copy(k, self.me).wait_send()
+
+        def item(self, q):
+            return self.held[pl.ds(q, self.slots, stride=self.slot), :]
+
+    ex_x = Exchange("gx", mx, peers_x, held_x, SLOT, ROWS, send_x, recv_x)
+    ex_y = Exchange("gy", my, peers_y, held_y, SUB, SUB, send_y, recv_y)
+    ex_f = Exchange("gy", my, peers_y, flow_y, SUB, 4, send_f, recv_f)
+
+    def my_ends(comp, me, x0, x1):
+        slots = x0.shape[0]
+        base = 2 * comp * slots
+        ends[pl.ds(base, slots), :] = x0
+        ends[pl.ds(base + slots, slots), :] = x1
+        return ends[pl.ds(me + base, 1), :], ends[pl.ds(me + base + slots, 1), :]
+
+    for load in loads[:3]:
         load.wait()
     mat_t[...] = material[...].T
+    jx = joints_x[...]
+    span = cols // SUB
+    along_x, mats = block_structure(conduct, mat_t, jx, mx * cols)
+    loads[3].wait()
     for comp in range(2):
         field_t[comp] = fields[comp].T
-    jx = joints_x[...]
-
-    span = cols // SUB
-    along_x = block_structure(conduct, mat_t, jx, mx * cols)
-    kept_x, parts = [], []
-    for comp in range(2):
-        inner, shared = along_x[comp]
+    kept_x, lines = [], list(mats)
+    for inner, shared in along_x:
+        comp = len(kept_x)
         kept, f0, f1 = block_source(
             inner, [field_t[comp, pl.ds(t, SUB, stride=span), :] for t in range(span)]
         )
         kept_x.append(kept)
-        parts.append(shared + (f0, f1))
-    publish(0, parts)
+        lines += list(shared) + [f0, f1]
+    ex_x.publish(lines)
     pl.semaphore_wait(barrier, nx + ny - 2)
-    for off in range(1, nx):
-        copy_to(0, off).start()
+    ex_x.start()
+
     loads[4].wait()
     jy = joints_y[...]
     span_y = rows // SUB
-    along_y = block_structure(conduct, material, jy, my * rows)
-    for off in range(1, nx):
-        copy_from(0, off).wait_recv()
-    found = gather_ends(0, jx, cols)
+    along_y, mats = block_structure(conduct, material, jy, my * rows)
+    ex_y.publish(list(mats) + list(along_y[0][1]) + list(along_y[1][1]))
+    ex_y.start()
+
+    ex_x.wait()
+    mats = [ex_x.item(q) for q in range(2)]
     for comp in range(2):
-        x = block_solve(along_x[comp][0], kept_x[comp], *found[comp])
+        b, g0, g1, f0, f1 = [ex_x.item(2 + 5 * comp + q) for q in range(5)]
+        structure = chain_structure(conduct, comp, (b, g0, g1), mats, jx, nx, cols)
+        found = my_ends(comp, mx, *chain_source(structure, f0, f1))
+        x = block_solve(along_x[comp][0], kept_x[comp], *found)
         for t in range(span):
             half_t[comp, pl.ds(t, SUB, stride=span), :] = x[t]
         half[comp] = half_t[comp].T
 
-    kept_y, parts = [], []
+    kept_y, lines = [], []
     for comp in range(2):
-        inner, shared = along_y[comp]
         kept, f0, f1 = block_source(
-            inner, [half[comp, pl.ds(t, SUB, stride=span_y), :] for t in range(span_y)]
+            along_y[comp][0],
+            [half[comp, pl.ds(t, SUB, stride=span_y), :] for t in range(span_y)],
         )
         kept_y.append(kept)
-        parts.append(shared + (f0, f1))
-    publish(1, parts)
-    for off in range(1, ny):
-        copy_to(1, off).start()
-    for off in range(1, ny):
-        copy_from(1, off).wait_recv()
-    found = gather_ends(1, jy, rows)
+        lines += [f0, f1]
+    ex_f.publish(lines)
+    ex_f.start()
+    ex_y.wait()
+    mats = [ex_y.item(q) for q in range(2)]
+    structures = [
+        chain_structure(
+            conduct, comp, [ex_y.item(2 + 3 * comp + q) for q in range(3)], mats, jy, ny, rows
+        )
+        for comp in range(2)
+    ]
+    ex_f.wait()
     for comp in range(2):
-        x = block_solve(along_y[comp][0], kept_y[comp], *found[comp])
+        f0, f1 = [ex_f.item(2 * comp + q) for q in range(2)]
+        found = my_ends(comp, my, *chain_source(structures[comp], f0, f1))
+        x = block_solve(along_y[comp][0], kept_y[comp], *found)
         for t in range(span_y):
             advanced[comp, pl.ds(t, SUB, stride=span_y), :] = x[t]
-    for off in range(1, nx):
-        copy_to(0, off).wait_send()
-    for off in range(1, ny):
-        copy_to(1, off).wait_send()
+    ex_x.finish()
+    ex_y.finish()
+    ex_f.finish()
 
 
 def write_out(half, advanced, half_out, advanced_out, sems):
@@ -345,10 +386,13 @@
             pltpu.VMEM((cols, rows), jnp.int32),
             pltpu.VMEM((2, cols, rows), jnp.float32),
             pltpu.VMEM((sx * SLOT, rows), jnp.float32),
-            pltpu.VMEM((sy * SLOT, cols), jnp.float32),
-            pltpu.VMEM((2 * max(sx, sy), cols), jnp.float32),
+            pltpu.VMEM((sy * SUB, cols), jnp.float32),
+            pltpu.VMEM((sy * SUB, cols), jnp.float32),
+            pltpu.VMEM((4 * max(sx, sy), cols), jnp.float32),
             pltpu.SemaphoreType.DMA((nx,)),
             pltpu.SemaphoreType.DMA((nx,)),
+            pltpu.SemaphoreType.DMA((ny,)),
+            pltpu.SemaphoreType.DMA((ny,)),
             pltpu.SemaphoreType.DMA((ny,)),
             pltpu.SemaphoreType.DMA((ny,)),
             pltpu.SemaphoreType.DMA((5,)),

time: 14.4 us -> 14.3 us (level)
  no operation moved by 1% of the time
where the time goes in v3:
time: 14.3 us; the launch traced here: 14.1 us
  Pallas kernels  13.5 us (94%)
  between operations  0.64 us (4%)
    pallas_call x1, Pallas kernels, per_device(): pl.pallas_call(kernel, out_shape=(shape, shape), in_specs=[hbm] * 5, out_...  12.8 us
    pallas_call x1, Pallas kernels, per_device(): pl.pallas_call(write_out, out_shape=(shape, shape), in_specs=[vmem, vmem]...  0.72 us

profile of v3, /device:TPU:0, one launch (start us, length us, event | category | flops | bytes accessed | tf_op | source)
XLA Modules:
  0.0 14.1 jit_solution(7654881176758121616)
XLA Ops:
  0.6 12.8 %shard_map.68 = (f32[2,128,128]{2,1,0:T(8,128)S(1)}, f32[2,128,128]{2,1,0:T(8,128)S(1)}) custom-call(f32[2,128,128]{2,1,0:T(8,128)} %fields_in.1, s32[128,128]{1,0:T(8,128)} %material_in.1, f32[2,8]{1,0:T(2,128)} %conduct_in.1, s32[8,128]{1,0:T(8,128)} %bitcast.2, s32[8,128]{1,0:T(8,128)} %bitcast.3), custom_call_target="tpu_custom_call" | custom-call | tf_op jit(solution)/shard_map/pallas_call | solution.py:374
  13.4 0.7 %shard_map.69 = (f32[2,128,128]{2,1,0:T(8,128)}, f32[2,128,128]{2,1,0:T(8,128)}) custom-call(f32[2,128,128]{2,1,0:T(8,128)S(1)} %get-tuple-element.4.half, f32[2,128,128]{2,1,0:T(8,128)S(1)} %get-tuple-element.5.advanced), custom_call_target="tpu_custom_call" | custom-call | tf_op jit(solution)/shard_map/pallas_call | solution.py:409

commit v4 on v3

--- a/solution.py
+++ b/solution.py
@@ -193,10 +193,16 @@
     return x0, x1
 
 
+def over(value, n):
+    if n & (n - 1):
+        return lax.div(value, n)
+    return lax.shift_right_arithmetic(value, n.bit_length() - 1)
+
+
 def far_first(me, n, k):
-    down = n - 1 - k - lax.div(me + k + 1, n)
-    up = k + lax.div(k - me + n, n)
-    half = lax.div(2 * me, n)
+    down = n - 1 - k - over(me + k + 1, n)
+    up = k + over(k - me + n, n)
+    half = over(2 * me, n)
     return half * up + (1 - half) * down
 
 
@@ -226,7 +232,7 @@
 
     barrier = pltpu.get_barrier_semaphore()
     peers_x = [far_first(mx, nx, k) for k in range(nx - 1)]
-    peers_y = [lax.rem(my + k, ny) for k in range(1, ny)]
+    peers_y = [my + k - ny * over(my + k, ny) for k in range(1, ny)]
     for axis, peers in (("gx", peers_x), ("gy", peers_y)):
         for peer in peers:
             pl.semaphore_signal(

time: 14.3 us -> 14.3 us (level)
  no operation moved by 1% of the time
where the time goes in v4:
time: 14.3 us; the launch traced here: 14.1 us
  Pallas kernels  13.5 us (94%)
  between operations  0.64 us (4%)
    pallas_call x1, Pallas kernels, per_device(): pl.pallas_call(kernel, out_shape=(shape, shape), in_specs=[hbm] * 5, out_...  12.8 us
    pallas_call x1, Pallas kernels, per_device(): pl.pallas_call(write_out, out_shape=(shape, shape), in_specs=[vmem, vmem]...  0.72 us

profile of v4, /device:TPU:0, one launch (start us, length us, event | category | flops | bytes accessed | tf_op | source)
XLA Modules:
  0.0 14.1 jit_solution(5011331606935025892)
XLA Ops:
  0.6 12.8 %shard_map.68 = (f32[2,128,128]{2,1,0:T(8,128)S(1)}, f32[2,128,128]{2,1,0:T(8,128)S(1)}) custom-call(f32[2,128,128]{2,1,0:T(8,128)} %fields_in.1, s32[128,128]{1,0:T(8,128)} %material_in.1, f32[2,8]{1,0:T(2,128)} %conduct_in.1, s32[8,128]{1,0:T(8,128)} %bitcast.2, s32[8,128]{1,0:T(8,128)} %bitcast.3), custom_call_target="tpu_custom_call" | custom-call | tf_op jit(solution)/shard_map/pallas_call | solution.py:380
  13.4 0.7 %shard_map.69 = (f32[2,128,128]{2,1,0:T(8,128)}, f32[2,128,128]{2,1,0:T(8,128)}) custom-call(f32[2,128,128]{2,1,0:T(8,128)S(1)} %get-tuple-element.4.half, f32[2,128,128]{2,1,0:T(8,128)S(1)} %get-tuple-element.5.advanced), custom_call_target="tpu_custom_call" | custom-call | tf_op jit(solution)/shard_map/pallas_call | solution.py:415

commit v5 on v4

--- a/solution.py
+++ b/solution.py
@@ -209,7 +209,7 @@
 def kernel(
     fields_in, material_in, conduct_in, joints_x_in, joints_y_in, half, advanced,
     fields, material, conduct, joints_x, joints_y,
-    field_t, mat_t, half_t, held_x, held_y, flow_y, ends,
+    field_t, mat_t, half_t, resp_x, resp_y, part_y, mix, held_x, held_y, flow_y, ends,
     send_x, recv_x, send_y, recv_y, send_f, recv_f, load_sem,
 ):
     nx, ny = lax.axis_size("gx"), lax.axis_size("gy")
@@ -318,27 +318,69 @@
     ex_y.publish(list(mats) + list(along_y[0][1]) + list(along_y[1][1]))
     ex_y.start()
 
+    zero = jnp.zeros((SUB, cols), jnp.float32)
+    one = jnp.ones((SUB, cols), jnp.float32)
+    none_x, none_y = ([zero] * span, zero), ([zero] * span_y, zero)
+
+    def keep(ref, index, values):
+        for t, value in enumerate(values):
+            ref[index, pl.ds(t, SUB, stride=len(values)), :] = value
+
+    for comp in range(2):
+        inner = along_x[comp][0]
+        for q, values in enumerate(
+            (
+                block_solve(inner, kept_x[comp], zero, zero),
+                block_solve(inner, none_x, one, zero),
+                block_solve(inner, none_x, zero, one),
+            )
+        ):
+            keep(resp_x, 3 * comp + q, values)
+        inner = along_y[comp][0]
+        for q, values in enumerate(
+            (block_solve(inner, none_y, one, zero), block_solve(inner, none_y, zero, one))
+        ):
+            keep(resp_y, 2 * comp + q, values)
+    base = []
+    for comp in range(2):
+        turned = [resp_x[3 * comp + q].T for q in range(3)]
+        for q in range(2):
+            weight = resp_y[2 * comp + q]
+            base.append(jnp.sum(weight * turned[0], axis=0, keepdims=True))
+            for p in range(2):
+                mix[comp, p * rows : (p + 1) * rows, q * cols : (q + 1) * cols] = (
+                    weight * turned[1 + p]
+                )
+
     ex_x.wait()
     mats = [ex_x.item(q) for q in range(2)]
+    found_x, lines = [], []
     for comp in range(2):
         b, g0, g1, f0, f1 = [ex_x.item(2 + 5 * comp + q) for q in range(5)]
         structure = chain_structure(conduct, comp, (b, g0, g1), mats, jx, nx, cols)
         found = my_ends(comp, mx, *chain_source(structure, f0, f1))
-        x = block_solve(along_x[comp][0], kept_x[comp], *found)
-        for t in range(span):
-            half_t[comp, pl.ds(t, SUB, stride=span), :] = x[t]
-        half[comp] = half_t[comp].T
-
-    kept_y, lines = [], []
-    for comp in range(2):
-        kept, f0, f1 = block_source(
-            along_y[comp][0],
-            [half[comp, pl.ds(t, SUB, stride=span_y), :] for t in range(span_y)],
-        )
-        kept_y.append(kept)
-        lines += [f0, f1]
+        found_x.append(found)
+        sides = jnp.broadcast_to(jnp.concatenate(found, axis=1), (SUB, 2 * rows))
+        flow = jnp.dot(
+            sides, mix[comp], precision=lax.Precision.HIGHEST,
+            preferred_element_type=jnp.float32,
+        )
+        for q in range(2):
+            lines.append(base[2 * comp + q] + flow[0:1, q * cols : (q + 1) * cols])
     ex_f.publish(lines)
     ex_f.start()
+
+    for comp in range(2):
+        first, last = found_x[comp]
+        half_t[comp] = (
+            resp_x[3 * comp] + resp_x[3 * comp + 1] * first + resp_x[3 * comp + 2] * last
+        )
+        half[comp] = half_t[comp].T
+        inner = along_y[comp][0]
+        kept, _, _ = block_source(
+            inner, [half[comp, pl.ds(t, SUB, stride=span_y), :] for t in range(span_y)]
+        )
+        keep(part_y, comp, block_solve(inner, kept, zero, zero))
     ex_y.wait()
     mats = [ex_y.item(q) for q in range(2)]
     structures = [
@@ -350,10 +392,10 @@
     ex_f.wait()
     for comp in range(2):
         f0, f1 = [ex_f.item(2 * comp + q) for q in range(2)]
-        found = my_ends(comp, my, *chain_source(structures[comp], f0, f1))
-        x = block_solve(along_y[comp][0], kept_y[comp], *found)
-        for t in range(span_y):
-            advanced[comp, pl.ds(t, SUB, stride=span_y), :] = x[t]
+        first, last = my_ends(comp, my, *chain_source(structures[comp], f0, f1))
+        advanced[comp] = (
+            part_y[comp] + resp_y[2 * comp] * first + resp_y[2 * comp + 1] * last
+        )
     ex_x.finish()
     ex_y.finish()
     ex_f.finish()
@@ -391,6 +433,10 @@
             pltpu.VMEM((2, cols, rows), jnp.float32),
             pltpu.VMEM((cols, rows), jnp.int32),
             pltpu.VMEM((2, cols, rows), jnp.float32),
+            pltpu.VMEM((6, cols, rows), jnp.float32),
+            pltpu.VMEM((4, rows, cols), jnp.float32),
+            pltpu.VMEM((2, rows, cols), jnp.float32),
+            pltpu.VMEM((2, 2 * rows, 2 * cols), jnp.float32),
             pltpu.VMEM((sx * SLOT, rows), jnp.float32),
             pltpu.VMEM((sy * SUB, cols), jnp.float32),
             pltpu.VMEM((sy * SUB, cols), jnp.float32),

time: 14.3 us -> 14.4 us (level)
  no operation moved by 1% of the time
where the time goes in v5:
time: 14.4 us; the launch traced here: 14.3 us
  Pallas kernels  13.6 us (94%)
  between operations  0.64 us (4%)
    pallas_call x1, Pallas kernels, per_device(): pl.pallas_call(kernel, out_shape=(shape, shape), in_specs=[hbm] * 5, out_...  12.9 us
    pallas_call x1, Pallas kernels, per_device(): pl.pallas_call(write_out, out_shape=(shape, shape), in_specs=[vmem, vmem]...  0.72 us

profile of v5, /device:TPU:0, one launch (start us, length us, event | category | flops | bytes accessed | tf_op | source)
XLA Modules:
  0.0 14.3 jit_solution(14970167676077258802)
XLA Ops:
  0.6 12.9 %shard_map.68 = (f32[2,128,128]{2,1,0:T(8,128)S(1)}, f32[2,128,128]{2,1,0:T(8,128)S(1)}) custom-call(f32[2,128,128]{2,1,0:T(8,128)} %fields_in.1, s32[128,128]{1,0:T(8,128)} %material_in.1, f32[2,8]{1,0:T(2,128)} %conduct_in.1, s32[8,128]{1,0:T(8,128)} %bitcast.2, s32[8,128]{1,0:T(8,128)} %bitcast.3), custom_call_target="tpu_custom_call" | custom-call | tf_op jit(solution)/shard_map/pallas_call | solution.py:422
  13.5 0.7 %shard_map.69 = (f32[2,128,128]{2,1,0:T(8,128)}, f32[2,128,128]{2,1,0:T(8,128)}) custom-call(f32[2,128,128]{2,1,0:T(8,128)S(1)} %get-tuple-element.4.half, f32[2,128,128]{2,1,0:T(8,128)S(1)} %get-tuple-element.5.advanced), custom_call_target="tpu_custom_call" | custom-call | tf_op jit(solution)/shard_map/pallas_call | solution.py:461

commit v6 on v5

--- a/solution.py
+++ b/solution.py
@@ -193,17 +193,19 @@
     return x0, x1
 
 
+def two_terms(x):
+    coarse = x.astype(jnp.bfloat16)
+    return coarse, (x - coarse.astype(jnp.float32)).astype(jnp.bfloat16)
+
+
 def over(value, n):
     if n & (n - 1):
         return lax.div(value, n)
     return lax.shift_right_arithmetic(value, n.bit_length() - 1)
 
 
-def far_first(me, n, k):
-    down = n - 1 - k - over(me + k + 1, n)
-    up = k + over(k - me + n, n)
-    half = over(2 * me, n)
-    return half * up + (1 - half) * down
+def low_first(me, n):
+    return [k + over(k - me + n, n) for k in range(n - 1)]
 
 
 def kernel(
@@ -231,8 +233,8 @@
         load.start()
 
     barrier = pltpu.get_barrier_semaphore()
-    peers_x = [far_first(mx, nx, k) for k in range(nx - 1)]
-    peers_y = [my + k - ny * over(my + k, ny) for k in range(1, ny)]
+    peers_x = low_first(mx, nx)
+    peers_y = low_first(my, ny)
     for axis, peers in (("gx", peers_x), ("gy", peers_y)):
         for peer in peers:
             pl.semaphore_signal(
@@ -348,9 +350,10 @@
             weight = resp_y[2 * comp + q]
             base.append(jnp.sum(weight * turned[0], axis=0, keepdims=True))
             for p in range(2):
-                mix[comp, p * rows : (p + 1) * rows, q * cols : (q + 1) * cols] = (
-                    weight * turned[1 + p]
-                )
+                coarse, fine = two_terms(weight * turned[1 + p])
+                at = (slice(p * rows, (p + 1) * rows), slice(q * cols, (q + 1) * cols))
+                mix[comp, 0, *at] = coarse
+                mix[comp, 1, *at] = fine
 
     ex_x.wait()
     mats = [ex_x.item(q) for q in range(2)]
@@ -360,13 +363,17 @@
         structure = chain_structure(conduct, comp, (b, g0, g1), mats, jx, nx, cols)
         found = my_ends(comp, mx, *chain_source(structure, f0, f1))
         found_x.append(found)
-        sides = jnp.broadcast_to(jnp.concatenate(found, axis=1), (SUB, 2 * rows))
-        flow = jnp.dot(
-            sides, mix[comp], precision=lax.Precision.HIGHEST,
-            preferred_element_type=jnp.float32,
-        )
+        sides = jnp.concatenate(found, axis=1)
+        coarse, fine = two_terms(sides)
+        row = lax.broadcasted_iota(jnp.int32, (16, 2 * rows), 0)
+        stack = jnp.where(row == 0, coarse.astype(jnp.float32), 0.0)
+        stack = jnp.where(row == 1, fine.astype(jnp.float32), stack).astype(jnp.bfloat16)
+        flow = sum(
+            jnp.dot(stack, mix[comp, p], preferred_element_type=jnp.float32) for p in range(2)
+        )
+        flow = flow[0:1, :] + flow[1:2, :]
         for q in range(2):
-            lines.append(base[2 * comp + q] + flow[0:1, q * cols : (q + 1) * cols])
+            lines.append(base[2 * comp + q] + flow[:, q * cols : (q + 1) * cols])
     ex_f.publish(lines)
     ex_f.start()
 
@@ -436,7 +443,7 @@
             pltpu.VMEM((6, cols, rows), jnp.float32),
             pltpu.VMEM((4, rows, cols), jnp.float32),
             pltpu.VMEM((2, rows, cols), jnp.float32),
-            pltpu.VMEM((2, 2 * rows, 2 * cols), jnp.float32),
+            pltpu.VMEM((2, 2, 2 * rows, 2 * cols), jnp.bfloat16),
             pltpu.VMEM((sx * SLOT, rows), jnp.float32),
             pltpu.VMEM((sy * SUB, cols), jnp.float32),
             pltpu.VMEM((sy * SUB, cols), jnp.float32),

time: 14.4 us -> 14.2 us (0.986)
  Pallas kernels: 13.6 us -> 13.4 us
    pallas_call x1, Pallas kernels: 12.9 us -> 12.7 us  [per_device(): pl.pallas_call(kernel, out_shape=(shape, shape), in_specs=[hbm] * 5, out_...]
where the time goes in v6:
time: 14.2 us; the launch traced here: 14.1 us
  Pallas kernels  13.4 us (94%)
  between operations  0.64 us (5%)
    pallas_call x1, Pallas kernels, per_device(): pl.pallas_call(kernel, out_shape=(shape, shape), in_specs=[hbm] * 5, out_...  12.7 us
    pallas_call x1, Pallas kernels, per_device(): pl.pallas_call(write_out, out_shape=(shape, shape), in_specs=[vmem, vmem]...  0.72 us

profile of v6, /device:TPU:0, one launch (start us, length us, event | category | flops | bytes accessed | tf_op | source)
XLA Modules:
  0.0 14.1 jit_solution(16798814207450557273)
XLA Ops:
  0.6 12.7 %shard_map.68 = (f32[2,128,128]{2,1,0:T(8,128)S(1)}, f32[2,128,128]{2,1,0:T(8,128)S(1)}) custom-call(f32[2,128,128]{2,1,0:T(8,128)} %fields_in.1, s32[128,128]{1,0:T(8,128)} %material_in.1, f32[2,8]{1,0:T(2,128)} %conduct_in.1, s32[8,128]{1,0:T(8,128)} %bitcast.2, s32[8,128]{1,0:T(8,128)} %bitcast.3), custom_call_target="tpu_custom_call" | custom-call | tf_op jit(solution)/shard_map/pallas_call | solution.py:429
  13.4 0.7 %shard_map.69 = (f32[2,128,128]{2,1,0:T(8,128)}, f32[2,128,128]{2,1,0:T(8,128)}) custom-call(f32[2,128,128]{2,1,0:T(8,128)S(1)} %get-tuple-element.4.half, f32[2,128,128]{2,1,0:T(8,128)S(1)} %get-tuple-element.5.advanced), custom_call_target="tpu_custom_call" | custom-call | tf_op jit(solution)/shard_map/pallas_call | solution.py:468

commit v7 on v6

--- a/solution.py
+++ b/solution.py
@@ -217,29 +217,32 @@
     nx, ny = lax.axis_size("gx"), lax.axis_size("gy")
     mx, my = lax.axis_index("gx"), lax.axis_index("gy")
     rows, cols = material.shape
-    loads = [
-        pltpu.make_async_copy(source, target, load_sem.at[i])
-        for i, (source, target) in enumerate(
-            (
-                (material_in, material),
-                (conduct_in, conduct),
-                (joints_x_in, joints_x),
-                (fields_in, fields),
-                (joints_y_in, joints_y),
-            )
-        )
-    ]
-    for load in loads:
-        load.start()
-
     barrier = pltpu.get_barrier_semaphore()
-    peers_x = low_first(mx, nx)
-    peers_y = low_first(my, ny)
-    for axis, peers in (("gx", peers_x), ("gy", peers_y)):
+    peers_x, peers_y = low_first(mx, nx), low_first(my, ny)
+
+    def greet(axis, peers):
         for peer in peers:
             pl.semaphore_signal(
                 barrier, inc=1, device_id={axis: peer}, device_id_type=pl.DeviceIdType.MESH
             )
+
+    def load(sem, source, target):
+        copy = pltpu.make_async_copy(source, target, load_sem.at[sem])
+        copy.start()
+        return copy
+
+    greet("gx", peers_x)
+    half_rows = rows // 2
+    upper, lower = pl.ds(0, half_rows), pl.ds(half_rows, half_rows)
+    early = [
+        load(0, material_in.at[upper], material.at[upper]),
+        load(1, material_in.at[lower], material.at[lower]),
+        load(2, conduct_in, conduct),
+        load(3, joints_x_in, joints_x),
+    ]
+    late = [load(4 + c, fields_in.at[c], fields.at[c]) for c in range(2)]
+    last_load = load(6, joints_y_in, joints_y)
+    greet("gy", peers_y)
 
     class Exchange:
         def __init__(self, axis, me, peers, held, slot, used, send, recv):
@@ -292,14 +295,14 @@
         ends[pl.ds(base + slots, slots), :] = x1
         return ends[pl.ds(me + base, 1), :], ends[pl.ds(me + base + slots, 1), :]
 
-    for load in loads[:3]:
-        load.wait()
+    for copy in early:
+        copy.wait()
     mat_t[...] = material[...].T
     jx = joints_x[...]
     span = cols // SUB
     along_x, mats = block_structure(conduct, mat_t, jx, mx * cols)
-    loads[3].wait()
-    for comp in range(2):
+    for comp in range(2):
+        late[comp].wait()
         field_t[comp] = fields[comp].T
     kept_x, lines = [], list(mats)
     for inner, shared in along_x:
@@ -313,7 +316,7 @@
     pl.semaphore_wait(barrier, nx + ny - 2)
     ex_x.start()
 
-    loads[4].wait()
+    last_load.wait()
     jy = joints_y[...]
     span_y = rows // SUB
     along_y, mats = block_structure(conduct, material, jy, my * rows)
@@ -454,7 +457,7 @@
             pltpu.SemaphoreType.DMA((ny,)),
             pltpu.SemaphoreType.DMA((ny,)),
             pltpu.SemaphoreType.DMA((ny,)),
-            pltpu.SemaphoreType.DMA((5,)),
+            pltpu.SemaphoreType.DMA((7,)),
         ],
         compiler_params=pltpu.CompilerParams(
             collective_id=0, has_side_effects=True, vmem_limit_bytes=16 * 1024 * 1024

time: 14.2 us -> 14.4 us (1.014)
  Pallas kernels: 13.4 us -> 13.6 us
    pallas_call x1, Pallas kernels: 12.7 us -> 12.9 us  [per_device(): pl.pallas_call(kernel, out_shape=(shape, shape), in_specs=[hbm] * 5, out_...]
where the time goes in v7:
time: 14.4 us; the launch traced here: 14.2 us
  Pallas kernels  13.6 us (94%)
  between operations  0.64 us (4%)
    pallas_call x1, Pallas kernels, per_device(): pl.pallas_call(kernel, out_shape=(shape, shape), in_specs=[hbm] * 5, out_...  12.9 us
    pallas_call x1, Pallas kernels, per_device(): pl.pallas_call(write_out, out_shape=(shape, shape), in_specs=[vmem, vmem]...  0.72 us

profile of v7, /device:TPU:0, one launch (start us, length us, event | category | flops | bytes accessed | tf_op | source)
XLA Modules:
  0.0 14.2 jit_solution(800376336626156203)
XLA Ops:
  0.6 12.9 %shard_map.68 = (f32[2,128,128]{2,1,0:T(8,128)S(1)}, f32[2,128,128]{2,1,0:T(8,128)S(1)}) custom-call(f32[2,128,128]{2,1,0:T(8,128)} %fields_in.1, s32[128,128]{1,0:T(8,128)} %material_in.1, f32[2,8]{1,0:T(2,128)} %conduct_in.1, s32[8,128]{1,0:T(8,128)} %bitcast.2, s32[8,128]{1,0:T(8,128)} %bitcast.3), custom_call_target="tpu_custom_call" | custom-call | tf_op jit(solution)/shard_map/pallas_call | solution.py:432
  13.5 0.7 %shard_map.69 = (f32[2,128,128]{2,1,0:T(8,128)}, f32[2,128,128]{2,1,0:T(8,128)}) custom-call(f32[2,128,128]{2,1,0:T(8,128)S(1)} %get-tuple-element.4.half, f32[2,128,128]{2,1,0:T(8,128)S(1)} %get-tuple-element.5.advanced), custom_call_target="tpu_custom_call" | custom-call | tf_op jit(solution)/shard_map/pallas_call | solution.py:471

commit v8 on v6

--- a/solution.py
+++ b/solution.py
@@ -211,7 +211,7 @@
 def kernel(
     fields_in, material_in, conduct_in, joints_x_in, joints_y_in, half, advanced,
     fields, material, conduct, joints_x, joints_y,
-    field_t, mat_t, half_t, resp_x, resp_y, part_y, mix, held_x, held_y, flow_y, ends,
+    field_t, mat_t, half_t, resp_x, resp_y, part_y, mix, saved, base, held_x, held_y, flow_y, ends,
     send_x, recv_x, send_y, recv_y, send_f, recv_f, load_sem,
 ):
     nx, ny = lax.axis_size("gx"), lax.axis_size("gy")
@@ -310,50 +310,72 @@
         kept_x.append(kept)
         lines += list(shared) + [f0, f1]
     ex_x.publish(lines)
-    pl.semaphore_wait(barrier, nx + ny - 2)
-    ex_x.start()
-
     loads[4].wait()
     jy = joints_y[...]
     span_y = rows // SUB
-    along_y, mats = block_structure(conduct, material, jy, my * rows)
-    ex_y.publish(list(mats) + list(along_y[0][1]) + list(along_y[1][1]))
-    ex_y.start()
-
     zero = jnp.zeros((SUB, cols), jnp.float32)
     one = jnp.ones((SUB, cols), jnp.float32)
-    none_x, none_y = ([zero] * span, zero), ([zero] * span_y, zero)
+    static = {}
 
     def keep(ref, index, values):
         for t, value in enumerate(values):
             ref[index, pl.ds(t, SUB, stride=len(values)), :] = value
 
-    for comp in range(2):
-        inner = along_x[comp][0]
-        for q, values in enumerate(
-            (
-                block_solve(inner, kept_x[comp], zero, zero),
-                block_solve(inner, none_x, one, zero),
-                block_solve(inner, none_x, zero, one),
-            )
-        ):
-            keep(resp_x, 3 * comp + q, values)
-        inner = along_y[comp][0]
-        for q, values in enumerate(
-            (block_solve(inner, none_y, one, zero), block_solve(inner, none_y, zero, one))
-        ):
-            keep(resp_y, 2 * comp + q, values)
-    base = []
-    for comp in range(2):
-        turned = [resp_x[3 * comp + q].T for q in range(3)]
-        for q in range(2):
-            weight = resp_y[2 * comp + q]
-            base.append(jnp.sum(weight * turned[0], axis=0, keepdims=True))
-            for p in range(2):
-                coarse, fine = two_terms(weight * turned[1 + p])
-                at = (slice(p * rows, (p + 1) * rows), slice(q * cols, (q + 1) * cols))
-                mix[comp, 0, *at] = coarse
-                mix[comp, 1, *at] = fine
+    def prepare():
+        along_y, mats = block_structure(conduct, material, jy, my * rows)
+        ex_y.publish(list(mats) + list(along_y[0][1]) + list(along_y[1][1]))
+
+        none_x, none_y = ([zero] * span, zero), ([zero] * span_y, zero)
+
+        for comp in range(2):
+            inner = along_x[comp][0]
+            for q, values in enumerate(
+                (
+                    block_solve(inner, kept_x[comp], zero, zero),
+                    block_solve(inner, none_x, one, zero),
+                    block_solve(inner, none_x, zero, one),
+                )
+            ):
+                keep(resp_x, 3 * comp + q, values)
+            inner = along_y[comp][0]
+            for q, values in enumerate(
+                (block_solve(inner, none_y, one, zero), block_solve(inner, none_y, zero, one))
+            ):
+                keep(resp_y, 2 * comp + q, values)
+        flat, kind = jax.tree.flatten([inner for inner, _ in along_y])
+        static.update(kind=kind, leaves=[x if isinstance(x, int) else None for x in flat])
+        for at, leaf in enumerate(flat):
+            if not isinstance(leaf, int):
+                saved[at] = leaf
+        for comp in range(2):
+            turned = [resp_x[3 * comp + q].T for q in range(3)]
+            for q in range(2):
+                weight = resp_y[2 * comp + q]
+                base[2 * comp + q : 2 * comp + q + 1, :] = jnp.sum(
+                    weight * turned[0], axis=0, keepdims=True
+                )
+                for p in range(2):
+                    coarse, fine = two_terms(weight * turned[1 + p])
+                    spot = (slice(p * rows, (p + 1) * rows), slice(q * cols, (q + 1) * cols))
+                    mix[comp, 0, *spot] = coarse
+                    mix[comp, 1, *spot] = fine
+
+
+    def send():
+        pl.semaphore_wait(barrier, nx + ny - 2)
+        ex_x.start()
+
+    late = over(2 * mx, nx)
+
+    def turn(step, carry):
+        pl.when(step == late)(prepare)
+        pl.when(step == 1 - late)(send)
+        return carry
+
+    lax.fori_loop(0, 2, turn, 0)
+    ex_y.start()
+    leaves = [saved[at] if x is None else x for at, x in enumerate(static["leaves"])]
+    inner_y = jax.tree.unflatten(static["kind"], leaves)
 
     ex_x.wait()
     mats = [ex_x.item(q) for q in range(2)]
@@ -373,7 +395,7 @@
         )
         flow = flow[0:1, :] + flow[1:2, :]
         for q in range(2):
-            lines.append(base[2 * comp + q] + flow[:, q * cols : (q + 1) * cols])
+            lines.append(base[2 * comp + q : 2 * comp + q + 1, :] + flow[:, q * cols : (q + 1) * cols])
     ex_f.publish(lines)
     ex_f.start()
 
@@ -383,7 +405,7 @@
             resp_x[3 * comp] + resp_x[3 * comp + 1] * first + resp_x[3 * comp + 2] * last
         )
         half[comp] = half_t[comp].T
-        inner = along_y[comp][0]
+        inner = inner_y[comp]
         kept, _, _ = block_source(
             inner, [half[comp, pl.ds(t, SUB, stride=span_y), :] for t in range(span_y)]
         )
@@ -444,6 +466,8 @@
             pltpu.VMEM((4, rows, cols), jnp.float32),
             pltpu.VMEM((2, rows, cols), jnp.float32),
             pltpu.VMEM((2, 2, 2 * rows, 2 * cols), jnp.bfloat16),
+            pltpu.VMEM((256, SUB, cols), jnp.float32),
+            pltpu.VMEM((SUB, cols), jnp.float32),
             pltpu.VMEM((sx * SLOT, rows), jnp.float32),
             pltpu.VMEM((sy * SUB, cols), jnp.float32),
             pltpu.VMEM((sy * SUB, cols), jnp.float32),

time: 14.2 us -> 14.2 us (level)
  no operation moved by 1% of the time
where the time goes in v8:
time: 14.2 us; the launch traced here: 14.1 us
  Pallas kernels  13.5 us (95%)
  between operations  0.64 us (5%)
    pallas_call x1, Pallas kernels, per_device(): pl.pallas_call(kernel, out_shape=(shape, shape), in_specs=[hbm] * 5, out_...  12.7 us
    pallas_call x1, Pallas kernels, per_device(): pl.pallas_call(write_out, out_shape=(shape, shape), in_specs=[vmem, vmem]...  0.72 us

profile of v8, /device:TPU:0, one launch (start us, length us, event | category | flops | bytes accessed | tf_op | source)
XLA Modules:
  0.0 14.1 jit_solution(11270654116292669081)
XLA Ops:
  0.6 12.7 %shard_map.68 = (f32[2,128,128]{2,1,0:T(8,128)S(1)}, f32[2,128,128]{2,1,0:T(8,128)S(1)}) custom-call(f32[2,128,128]{2,1,0:T(8,128)} %fields_in.1, s32[128,128]{1,0:T(8,128)} %material_in.1, f32[2,8]{1,0:T(2,128)} %conduct_in.1, s32[8,128]{1,0:T(8,128)} %bitcast.2, s32[8,128]{1,0:T(8,128)} %bitcast.3), custom_call_target="tpu_custom_call" | custom-call | tf_op jit(solution)/shard_map/pallas_call | solution.py:451
  13.4 0.7 %shard_map.69 = (f32[2,128,128]{2,1,0:T(8,128)}, f32[2,128,128]{2,1,0:T(8,128)}) custom-call(f32[2,128,128]{2,1,0:T(8,128)S(1)} %get-tuple-element.4.half, f32[2,128,128]{2,1,0:T(8,128)S(1)} %get-tuple-element.5.advanced), custom_call_target="tpu_custom_call" | custom-call | tf_op jit(solution)/shard_map/pallas_call | solution.py:492
